TPU v7x, 32 devices: a whole 2x2x4 slice. The times are simulated.
32 devices in a mesh: parts: 2 (over y), band: 16 (over z, x, core).
Axes of the slice: x: 2, y: 2, z: 4, core: 2. Of those that a mesh axis runs over, the one named last changes fastest.
Arguments:
- sky_image: bfloat16 [8192, 16384], P(('parts', 'band')), parts along dimension 0, may hold values from -6 to 6
- tile_band: int32 [2048, 1], P(('parts', 'band')), parts along dimension 0, may hold values from 0 to 15; in each aligned block of 64 rows (0 to 63, 64 to 127, ...) at most 8 rows name the same one
- tile_place: int32 [2048], P(('parts', 'band')), parts along dimension 0, may hold values from 0 to 2047
- counts: int32 [32, 64], P(('parts', 'band')), parts along dimension 0, may hold values from 1 to 128, 4096 in all within a row
- kernel: bfloat16 [2048, 128, 128], P(('parts', 'band')), parts along dimension 0, may hold values from -1.5 to 1.5
- observed: bfloat16 [2048, 2, 128], P(('parts', 'band')), parts along dimension 0, may hold values from -24 to 24
Outputs:
- gradient: bfloat16 [8192, 16384], P(('parts', 'band')), parts along dimension 0
There are 2 independent parts, one for each index of `parts`. A program takes and returns all parts, laid end to end along the dimension named above; each array names one. Nothing has to cross between parts.
Inputs may be any that keep to these rules, and one draw needn't show every extreme that they name: `tile_band`: no band is named by more than 8 slots of one index of band, and some index of band names one band exactly 8 times. The 64 counts of one index of band sum to 4096, the largest exactly 128.
All inputs are finite; a program needn't handle non-finite values.
Results may differ from a plain program's by a relative error of at most 0.015.
Values may be sent and summed in bfloat16 or wider, within the bound.
No kernel may reach another device: no remote copies, remote signals or barrier semaphores. Data moves between devices by JAX's collectives and lax.ppermute only.
A program may use at most 512 MiB of HBM per device.

v0:
```python
import math

import jax
import jax.numpy as jnp
from jax import lax
from jax.sharding import PartitionSpec as P

RADIX = 128
FACET = 4096
TILE = 64
VIS_SLOT = 128


def contract(pattern, table_part, data_part):
    return jnp.einsum(pattern, table_part, data_part, preferred_element_type=jnp.float32)


def dft_tables(orient):
    table_index = jnp.arange(RADIX, dtype=jnp.int32)
    product = table_index[:, None] * table_index[None, :] % RADIX
    table_angle = product.astype(jnp.float32) * (2.0 * math.pi / RADIX)
    return (
        jnp.cos(table_angle).astype(jnp.bfloat16),
        (orient * jnp.sin(table_angle)).astype(jnp.bfloat16),
    )


def twiddle(orient):
    table_index = jnp.arange(RADIX, dtype=jnp.int32)
    product = table_index[:, None] * table_index[None, :]
    table_angle = product.astype(jnp.float32) * (2.0 * math.pi / (RADIX * RADIX))
    return (jnp.cos(table_angle), orient * jnp.sin(table_angle))


def along_last(part_real, part_imag, orient, used_in, used_out, real_out):
    cos_table, sin_table = dft_tables(orient)
    twist_cos, twist_sin = twiddle(orient)
    batch_rows = part_real.shape[0]
    head_cos = cos_table[:, :used_in]
    head_sin = sin_table[:, :used_in]
    real_cube = part_real.reshape(batch_rows, used_in, RADIX)
    first_real = contract("kn,bnm->bkm", head_cos, real_cube)
    first_imag = contract("kn,bnm->bkm", head_sin, real_cube)
    if part_imag is not None:
        imag_cube = part_imag.reshape(batch_rows, used_in, RADIX)
        first_real = first_real - contract("kn,bnm->bkm", head_sin, imag_cube)
        first_imag = first_imag + contract("kn,bnm->bkm", head_cos, imag_cube)
    middle_real = ((first_real * twist_cos - first_imag * twist_sin) / RADIX).astype(jnp.bfloat16)
    middle_imag = ((first_real * twist_sin + first_imag * twist_cos) / RADIX).astype(jnp.bfloat16)
    tail_cos = cos_table[:used_out]
    tail_sin = sin_table[:used_out]
    final_real = contract("jm,bkm->bjk", tail_cos, middle_real) - contract(
        "jm,bkm->bjk", tail_sin, middle_imag
    )
    final_real = final_real.reshape(batch_rows, used_out * RADIX)
    if real_out:
        return final_real
    final_imag = contract("jm,bkm->bjk", tail_cos, middle_imag) + contract(
        "jm,bkm->bjk", tail_sin, middle_real
    )
    return (final_real, final_imag.reshape(batch_rows, used_out * RADIX))


def slot_gradient(tile_real, tile_imag, kernel, observed, counts):
    kernel_v = kernel[:, :, :TILE]
    kernel_u = kernel[:, :, TILE:]
    inner_real = contract("sab,sjb->sja", tile_real, kernel_u)
    inner_imag = contract("sab,sjb->sja", tile_imag, kernel_u)
    model_real = jnp.sum(kernel_v * inner_real, axis=2)
    model_imag = jnp.sum(kernel_v * inner_imag, axis=2)
    live_mask = jnp.arange(VIS_SLOT, dtype=jnp.int32)[None, :] < counts[:, None]
    resid_real = jnp.where(
        live_mask, observed[:, 0].astype(jnp.float32) - model_real, jnp.zeros_like(model_real)
    )
    resid_imag = jnp.where(
        live_mask, observed[:, 1].astype(jnp.float32) - model_imag, jnp.zeros_like(model_imag)
    )
    weighted_real = (kernel_v * resid_real[:, :, None]).astype(jnp.bfloat16)
    weighted_imag = (kernel_v * resid_imag[:, :, None]).astype(jnp.bfloat16)
    grad_real = contract("sja,sjb->sab", weighted_real, kernel_u)
    grad_imag = contract("sja,sjb->sab", weighted_imag, kernel_u)
    return (grad_real, grad_imag)


def on_device(sky_image, tile_band, tile_place, counts, kernel, observed):
    band_count = lax.axis_size("band")
    side_cells = sky_image.shape[1]
    half_cells = side_cells // 2
    band_cols = half_cells // band_count
    tiles_across = band_cols // TILE
    tile_total = side_cells // TILE * tiles_across
    facet_blocks = FACET // RADIX
    spec_real, spec_imag = along_last(sky_image, None, -1.0, RADIX, RADIX // 2, False)
    spectrum = jnp.stack([spec_real, spec_imag]).astype(jnp.bfloat16)
    columns = lax.all_to_all(spectrum, "band", split_axis=2, concat_axis=1, tiled=True)
    columns = columns.transpose(0, 2, 1)
    grid_real, grid_imag = along_last(columns[0], columns[1], -1.0, facet_blocks, RADIX, False)
    model_grid = jnp.stack([grid_real, grid_imag]).astype(jnp.bfloat16)
    tile_view = model_grid.reshape(2, tiles_across, TILE, side_cells // TILE, TILE)
    tile_view = tile_view.transpose(0, 3, 1, 4, 2).reshape(2, tile_total, TILE, TILE)
    owner_band = tile_band[:, 0]
    slots_here = owner_band.shape[0]
    capacity = max(2, (2 * slots_here + band_count - 1) // band_count)
    buffer_len = band_count * capacity
    onehot = (owner_band[:, None] == jnp.arange(band_count, dtype=jnp.int32)[None, :]).astype(
        jnp.int32
    )
    slot_rank = jnp.sum(jnp.cumsum(onehot, axis=0) * onehot, axis=1) - 1
    slot_pos = owner_band * capacity + slot_rank
    slot_counts = counts[0]
    empty_grad = jnp.zeros((2, tile_total, TILE, TILE), jnp.float32)
    request = jnp.zeros((buffer_len,), jnp.int32).at[slot_pos].set(tile_place)
    asked = lax.all_to_all(
        request.reshape(band_count, capacity), "band", split_axis=0, concat_axis=0, tiled=True
    )
    asked_flat = asked.reshape(buffer_len)
    served = tile_view[:, asked_flat].reshape(2, band_count, capacity, TILE, TILE)
    fetched = lax.all_to_all(served, "band", split_axis=1, concat_axis=1, tiled=True)
    my_tiles = fetched.reshape(2, buffer_len, TILE, TILE)[:, slot_pos]
    grad_real, grad_imag = slot_gradient(my_tiles[0], my_tiles[1], kernel, observed, slot_counts)
    returned = jnp.zeros((2, buffer_len, TILE, TILE), jnp.float32)
    returned = returned.at[:, slot_pos].set(jnp.stack([grad_real, grad_imag]))
    arrived = lax.all_to_all(
        returned.reshape(2, band_count, capacity, TILE, TILE).astype(jnp.bfloat16),
        "band",
        split_axis=1,
        concat_axis=1,
        tiled=True,
    ).astype(jnp.float32)
    grad_view = empty_grad.at[:, asked_flat].add(arrived.reshape(2, buffer_len, TILE, TILE))
    grad_band = grad_view.reshape(2, side_cells // TILE, tiles_across, TILE, TILE)
    grad_band = (
        grad_band.transpose(0, 2, 4, 1, 3).reshape(2, band_cols, side_cells).astype(jnp.bfloat16)
    )
    back_real, back_imag = along_last(grad_band[0], grad_band[1], 1.0, RADIX, facet_blocks, False)
    back_stack = jnp.stack([back_real, back_imag]).astype(jnp.bfloat16).transpose(0, 2, 1)
    image_cols = lax.all_to_all(back_stack, "band", split_axis=1, concat_axis=2, tiled=True)
    gradient = along_last(image_cols[0], image_cols[1], 1.0, RADIX // 2, RADIX, True)
    return gradient.astype(jnp.bfloat16)


def solution(mesh):
    return jax.shard_map(
        on_device,
        mesh=mesh,
        in_specs=(
            P(("parts", "band"), None),
            P(("parts", "band"), None),
            P(("parts", "band")),
            P(("parts", "band"), None),
            P(("parts", "band"), None, None),
            P(("parts", "band"), None, None),
        ),
        out_specs=P(("parts", "band"), None),
        check_vma=False,
    )
```

profile of v0, /device:TPU:0, one launch (start us, length us, event | category | flops | bytes accessed | tf_op | source)
XLA Modules:
  0.0 1874.9 jit_solution(4506451944753026451)
XLA Ops:
  74.8 17.9 copy.211
  110.8 17.7 copy.212
  128.5 19.8 %pad_maximum_fusion = bf16[2,256,8192]{1,0,2:T(2,128)(2,1)} fusion(bf16[1,256,8192]{1,0,2:T(2,128)(2,1)} %copy.212, bf16[1,256,8192]{1,0,2:T(2,128)(2,1)} %copy.211), kind=kLoop, calls=%fused_computation.48 | loop fusion | flops 16777216 | bytes 16777216 | tf_op jit(solution)/shard_map/stack | solution.py:94
  157.4 148.1 %all-to-all-done.1 = bf16[2,256,8192]{1,0,2:T(2,128)(2,1)} async-done(((bf16[2,256,8192]{1,0,2:T(2,128)(2,1)}), bf16[2,256,8192]{1,0,2:T(2,128)(2,1)}, u32[]{:S(2)}, u32[]{:S(2)}) %all-to-all-start.1) | async-done | bytes 8388640 | tf_op jit(solution)/shard_map/all_to_all | solution.py:95
  376.2 46.5 %fusion.8 = (bf16[512,128,128]{1,2,0:T(8,128)(2,1)}, bf16[512,128,128]{1,2,0:T(8,128)(2,1)}) fusion(f32[128,128]{0,1:T(8,128)S(1)} %copy.219, f32[128,128]{0,1:T(8,128)S(1)} %copy.216, f32[512,128,128]{2,1,0:T(8,128)} %fusion.85, f32[512,128,128]{2,1,0:T(8,128)} %fusion.86, f32[512,128,128]{2,1,0:T(8,128)} %fusion.88, bf16[512,32,128]{2,1,0:T(8,128)(2,1)} %bitcast.296, ...), kind=kOutput, calls=%fused_computation.20 | convolution fusion | flops 637534208 | bytes 138575872 | tf_op jit(solution)/shard_map/kn,bnm->bkm/dot_general | solution.py:15
  456.2 23.8 %fusion.12 = bf16[512,128,128]{1,2,0:T(8,128)(2,1)} fusion(f32[512,128,128]{2,1,0:T(8,128)} %fusion.75, bf16[512,128,128]{1,2,0:T(8,128)(2,1)} %get-tuple-element.8), kind=kOutput, calls=%fused_computation.28 | convolution fusion | flops 2164523008 | bytes 67108864 | tf_op jit(solution)/shard_map/jm,bkm->bjk/dot_general | solution.py:15
  480.0 22.5 %copy.222 = bf16[512,128,128]{2,1,0:T(8,128)(2,1)} copy(bf16[512,128,128]{1,2,0:T(8,128)(2,1)} %fusion.12) | data formatting | bytes 33554432 | tf_op jit(solution)/shard_map/sub | solution.py:52
  502.5 40.9 %stack.25 = bf16[1,8,64,256,64]{4,3,2,1,0:T(8,128)(2,1)} reshape(bf16[512,128,128]{2,1,0:T(8,128)(2,1)} %copy.222) | data formatting | bytes 33554432 | tf_op jit(solution)/shard_map/stack | solution.py:98
  543.3 23.9 %fusion.13 = bf16[512,128,128]{1,2,0:T(8,128)(2,1)} fusion(f32[512,128,128]{2,1,0:T(8,128)} %fusion.73, bf16[512,128,128]{1,2,0:T(8,128)(2,1)} %get-tuple-element.7), kind=kOutput, calls=%fused_computation.29 | convolution fusion | flops 2164523008 | bytes 67108864 | tf_op jit(solution)/shard_map/jm,bkm->bjk/dot_general | solution.py:15
  567.2 22.4 %copy.225 = bf16[512,128,128]{2,1,0:T(8,128)(2,1)} copy(bf16[512,128,128]{1,2,0:T(8,128)(2,1)} %fusion.13) | data formatting | bytes 33554432 | tf_op jit(solution)/shard_map/add | solution.py:58
  589.6 40.8 %stack.26 = bf16[1,8,64,256,64]{4,3,2,1,0:T(8,128)(2,1)} reshape(bf16[512,128,128]{2,1,0:T(8,128)(2,1)} %copy.225) | data formatting | bytes 33554432 | tf_op jit(solution)/shard_map/stack | solution.py:98
  630.4 44.3 %maximum_bitcast_fusion = bf16[2,256,8,64,64]{3,1,4,2,0:T(8,128)(2,1)} fusion(bf16[1,8,64,256,64]{4,3,2,1,0:T(8,128)(2,1)} %stack.26, bf16[1,8,64,256,64]{4,3,2,1,0:T(8,128)(2,1)} %stack.25), kind=kLoop, calls=%fused_computation.5 | loop fusion | flops 16777216 | bytes 67108864 | tf_op jit(solution)/shard_map/transpose | solution.py:100
  674.7 84.8 %copy.226 = bf16[2,256,8,64,64]{4,3,2,1,0:T(8,128)(2,1)} copy(bf16[2,256,8,64,64]{3,1,4,2,0:T(8,128)(2,1)} %maximum_bitcast_fusion) | data formatting | bytes 67108864 | tf_op jit(solution)/shard_map/transpose | solution.py:100
  777.9 38.8 %all-to-all-start.2 = ((bf16[16,2,32768]{2,1,0:T(2,128)(2,1)}), bf16[16,2,32768]{2,1,0:T(2,128)(2,1)}, u32[]{:S(2)}, u32[]{:S(2)}) async-start(bf16[16,2,32768]{2,1,0:T(2,128)(2,1)} %reshape.265), calls=%async_computation.2 | async-start | bytes 4194304 | tf_op jit(solution)/shard_map/all_to_all | solution.py:118
  817.8 40.1 %all-to-all-done.2 = bf16[16,2,32768]{2,1,0:T(2,128)(2,1)} async-done(((bf16[16,2,32768]{2,1,0:T(2,128)(2,1)}), bf16[16,2,32768]{2,1,0:T(2,128)(2,1)}, u32[]{:S(2)}, u32[]{:S(2)}) %all-to-all-start.2) | async-done | bytes 2097184 | tf_op jit(solution)/shard_map/all_to_all | solution.py:118
  929.6 39.3 %all-to-all-done.3 = bf16[16,2,32768]{2,1,0:T(2,128)(2,1)S(1)} async-done(((bf16[16,2,32768]{2,1,0:T(2,128)(2,1)}), bf16[16,2,32768]{2,1,0:T(2,128)(2,1)S(1)}, u32[]{:S(2)}, u32[]{:S(2)}) %all-to-all-start.3) | async-done | bytes 2097184 | tf_op jit(solution)/shard_map/all_to_all | solution.py:123
  981.3 41.3 %broadcast_in_dim.4 = f32[2,2048,64,64]{3,2,1,0:T(8,128)} broadcast(f32[]{:T(128)} %constant.50.clone.1), dimensions={} | broadcast | bytes 67108864 | tf_op jit(solution)/shard_map/broadcast_in_dim | solution.py:111
  1022.6 26.9 %scatter_fusion.1 = f32[2,2048,64,64]{3,2,1,0:T(8,128)} fusion(f32[2,2048,64,64]{3,2,1,0:T(8,128)} %broadcast_in_dim.4, s32[128]{0:T(128)S(1)} %copy-done.15, f32[128,2,64,64]{3,2,1,0:T(8,128)} %copy.234), kind=kCustom, calls=%fused_computation.4 | custom fusion | flops 1048576 | bytes 12583424 | tf_op jit(solution)/shard_map/scatter-add | solution.py:130
  1049.5 63.8 %convert_element_type.285 = bf16[2,2048,64,64]{3,2,1,0:T(8,128)(2,1)} convert(f32[2,2048,64,64]{3,2,1,0:T(8,128)} %scatter_fusion.1) | non-fusion elementwise | flops 16777216 | bytes 100663296 | tf_op jit(solution)/shard_map/convert_element_type | solution.py:133
  1113.3 44.2 %fusion.152 = (bf16[1,8,64,256,64]{2,4,1,3,0:T(8,128)(2,1)}, bf16[1,8,64,256,64]{2,4,1,3,0:T(8,128)(2,1)}) fusion(bf16[2,8,64,256,64]{2,4,1,3,0:T(8,128)(2,1)} %bitcast.44), kind=kLoop, calls=%fused_computation.215 | loop fusion | bytes 67108864 | tf_op jit(solution)/shard_map/slice | solution.py:135
  1157.5 42.7 %copy.237 = bf16[1,8,64,256,64]{4,3,2,1,0:T(8,128)(2,1)} copy(bf16[1,8,64,256,64]{2,4,1,3,0:T(8,128)(2,1)} %get-tuple-element.9) | data formatting | bytes 33554432 | tf_op jit(solution)/shard_map/slice | solution.py:135
  1200.3 41.8 %reshape_squeeze.21 = bf16[512,128,128]{2,1,0:T(8,128)(2,1)} reshape(bf16[1,8,64,256,64]{4,3,2,1,0:T(8,128)(2,1)} %copy.237) | data formatting | bytes 33554432 | tf_op jit(solution)/shard_map/reshape;squeeze | solution.py:45
  1275.5 42.2 %copy.235 = bf16[1,8,64,256,64]{4,3,2,1,0:T(8,128)(2,1)} copy(bf16[1,8,64,256,64]{2,4,1,3,0:T(8,128)(2,1)} %get-tuple-element.10) | data formatting | bytes 33554432 | tf_op jit(solution)/shard_map/slice | solution.py:135
  1317.7 42.1 %reshape_squeeze.20 = bf16[512,128,128]{2,1,0:T(8,128)(2,1)} reshape(bf16[1,8,64,256,64]{4,3,2,1,0:T(8,128)(2,1)} %copy.235) | data formatting | bytes 33554432 | tf_op jit(solution)/shard_map/reshape;squeeze | solution.py:41
  1359.8 16.8 fusion.71
  1376.7 50.0 %fusion.2 = (bf16[512,128,128]{1,2,0:T(8,128)(2,1)}, bf16[512,128,128]{1,2,0:T(8,128)(2,1)}) fusion(f32[128,128]{0,1:T(8,128)S(1)} %copy-done.7, f32[128,128]{0,1:T(8,128)S(1)} %copy-done.6, f32[512,128,128]{2,1,0:T(8,128)} %fusion.69, f32[512,128,128]{2,1,0:T(8,128)} %fusion.71, f32[512,128,128]{2,1,0:T(8,128)} %fusion.62, ...), kind=kOutput, calls=%fused_computation.10 | convolution fusion | flops 2248392704 | bytes 151126016 | tf_op jit(solution)/shard_map/kn,bnm->bkm/dot_general | solution.py:15
  1459.3 19.1 %copy.246 = bf16[1,512,4096]{1,0,2:T(2,128)(2,1)} copy(bf16[1,512,4096]{2,1,0:T(8,128)(2,1)} %stack_reshape.20) | data formatting | bytes 8388608 | tf_op jit(solution)/shard_map/stack;reshape | solution.py:136
  1498.2 18.8 %copy.247 = bf16[1,512,4096]{1,0,2:T(2,128)(2,1)} copy(bf16[1,512,4096]{2,1,0:T(8,128)(2,1)} %stack_reshape.21) | data formatting | bytes 8388608 | tf_op jit(solution)/shard_map/stack;reshape | solution.py:136
  1516.9 18.9 %maximum_bitcast_fusion.1 = bf16[2,4096,512]{2,0,1:T(2,128)(2,1)S(1)} fusion(bf16[1,512,4096]{1,0,2:T(2,128)(2,1)} %copy.247, bf16[1,512,4096]{1,0,2:T(2,128)(2,1)} %copy.246), kind=kLoop, calls=%fused_computation.49 | loop fusion | flops 16777216 | bytes 16777216 | tf_op jit(solution)/shard_map/transpose | solution.py:136
  1535.9 195.1 %all_to_all.52 = bf16[2,4096,512]{2,0,1:T(2,128)(2,1)} all-to-all(bf16[2,4096,512]{2,0,1:T(2,128)(2,1)S(1)} %maximum_bitcast_fusion.1), channel_id=1, replica_groups=mesh['parts'=2,'band'=16] {'band'}, dimensions={1} | all-to-all | bytes 16777216 | tf_op jit(solution)/shard_map/all_to_all | solution.py:137
  1808.2 19.7 %fusion.23 = f32[256,128,128]{2,1,0:T(8,128)} fusion(f32[256,128,128]{2,1,0:T(8,128)} %convolution_add_fusion, f32[256,128,128]{2,1,0:T(8,128)} %convolution_subtract_fusion, f32[128,128]{0,1:T(8,128)S(1)} %copy-done.7, f32[128,128]{0,1:T(8,128)S(1)} %copy-done.6), kind=kOutput, calls=%fused_computation.47 | convolution fusion | flops 1094959104 | bytes 50462720 | tf_op jit(solution)/shard_map/jm,bkm->bjk/dot_general | solution.py:15
  1827.9 21.4 %fusion.31 = bf16[256,128,128]{1,2,0:T(8,128)(2,1)} fusion(f32[256,128,128]{2,1,0:T(8,128)} %fusion.23, f32[256,128,128]{2,1,0:T(8,128)} %convolution_add_fusion, f32[256,128,128]{2,1,0:T(8,128)} %convolution_subtract_fusion, f32[128,128]{0,1:T(8,128)S(1)} %copy-done.7, f32[128,128]{0,1:T(8,128)S(1)} %copy-done.6), kind=kOutput, calls=%fused_computation.61 | convolution fusion | flops 1103347712 | bytes 58851328 | tf_op jit(solution)/shard_map/jm,bkm->bjk/dot_general | solution.py:15
  (124 shorter events, 498.3 us)
Async XLA Ops:
  2.3 19.1 %copy-start.12 = (s32[64]{0:T(128)}, s32[64]{0:T(128)S(1)}, u32[]{:S(2)}) copy-start(s32[64]{0:T(128)S(1)} %fusion.95) | copy-start | bytes 772
  3.9 144.4 %all-to-all-start = ((s32[16,1,8]{2,1,0:T(1,128)}), s32[16,1,8]{2,1,0:T(1,128)S(1)}, u32[]{:S(2)}, u32[]{:S(2)}) async-start(s32[16,1,8]{2,1,0:T(1,128)} %bitcast.3), calls=%async_computation | async-start | bytes 16384 | tf_op jit(solution)/shard_map/all_to_all | solution.py:113
  11.8 350.0 %copy-start.8 = (bf16[128,128]{1,0:T(8,128)(2,1)}, bf16[128,128]{1,0:T(8,128)(2,1)S(1)}, u32[]{:S(2)}) copy-start(bf16[128,128]{1,0:T(8,128)(2,1)S(1)} %cosine_convert_fusion) | copy-start | bytes 98308
  49.6 6.6 slice-start
  49.6 6.6 slice-start.1
  148.3 157.2 %all-to-all-start.1 = ((bf16[2,256,8192]{1,0,2:T(2,128)(2,1)}), bf16[2,256,8192]{1,0,2:T(2,128)(2,1)}, u32[]{:S(2)}, u32[]{:S(2)}) async-start(bf16[2,256,8192]{1,0,2:T(2,128)(2,1)} %pad_maximum_fusion), calls=%async_computation.1 | async-start | bytes 16777216 | tf_op jit(solution)/shard_map/all_to_all | solution.py:95
  154.9 221.3 %copy-start.5 = (f32[128,128]{0,1:T(8,128)}, f32[128,128]{0,1:T(8,128)S(1)}, u32[]{:S(2)}) copy-start(f32[128,128]{0,1:T(8,128)S(1)} %copy.216) | copy-start | bytes 196612
  156.3 0.5 copy-start.14
  361.8 2.0 copy-start.3
  764.6 52.1 %copy-start.4 = (bf16[64,128,128]{2,1,0:T(8,128)(2,1)S(1)}, bf16[64,128,128]{2,1,0:T(8,128)(2,1)}, u32[]{:S(2)}) copy-start(bf16[64,128,128]{2,1,0:T(8,128)(2,1)} %param.10) | copy-start | bytes 6291460
  770.4 47.3 %copy-start.13 = (s32[64]{0:T(128)S(1)}, s32[64]{0:T(128)}, u32[]{:S(2)}) copy-start(s32[64]{0:T(128)} %copy-done.12) | copy-start | bytes 772
  770.4 47.3 %copy-start.11 = (bf16[64,2,128]{2,1,0:T(2,128)(2,1)S(1)}, bf16[64,2,128]{2,1,0:T(2,128)(2,1)}, u32[]{:S(2)}) copy-start(bf16[64,2,128]{2,1,0:T(2,128)(2,1)} %param.11) | copy-start | bytes 98308
  777.9 79.9 %all-to-all-start.2 = ((bf16[16,2,32768]{2,1,0:T(2,128)(2,1)}), bf16[16,2,32768]{2,1,0:T(2,128)(2,1)}, u32[]{:S(2)}, u32[]{:S(2)}) async-start(bf16[16,2,32768]{2,1,0:T(2,128)(2,1)} %reshape.265), calls=%async_computation.2 | async-start | bytes 4194304 | tf_op jit(solution)/shard_map/all_to_all | solution.py:118
  870.9 9.2 copy-start.16
  916.4 52.5 %all-to-all-start.3 = ((bf16[16,2,32768]{2,1,0:T(2,128)(2,1)}), bf16[16,2,32768]{2,1,0:T(2,128)(2,1)S(1)}, u32[]{:S(2)}, u32[]{:S(2)}) async-start(bf16[16,2,32768]{2,1,0:T(2,128)(2,1)} %reshape.267), calls=%async_computation.3 | async-start | bytes 4194304 | tf_op jit(solution)/shard_map/all_to_all | solution.py:123
  981.3 41.3 %copy-start.15 = (s32[128]{0:T(128)S(1)}, s32[128]{0:T(128)}, u32[]{:S(2)}) copy-start(s32[128]{0:T(128)} %copy-done.14) | copy-start | bytes 1540
  1359.8 16.8 copy-start.6
  1359.8 16.8 copy-start.7
  1376.7 50.0 %copy-start.9 = (bf16[128,128]{1,0:T(8,128)(2,1)S(1)}, bf16[128,128]{1,0:T(8,128)(2,1)}, u32[]{:S(2)}) copy-start(bf16[128,128]{1,0:T(8,128)(2,1)} %copy-done.8) | copy-start | bytes 98308
  1426.7 10.5 copy-start
  1437.2 4.6 copy-start.10
  1756.0 10.5 copy-start.2
  1781.2 16.6 copy-start.1
where the time goes:
time: 1900 us; the launch traced here: 1870 us
  local copies, waits for them, and re-layouts  756 us (40%)
  matrix products  447 us (24%)
  waiting for transfers between devices  227 us (12%)
  blocking collectives  195 us (10%)
  other arithmetic  185 us (10%)
  starting transfers between devices  64 us (3%)
    dot_general x32, matrix products, contract(): jnp.einsum(pattern, table_part, data_part, preferred_element_type=jnp.flo...  447 us
    all_to_all x1, blocking collectives, on_device(): lax.all_to_all(back_stack, 'band', split_axis=1, concat_axis=2, tiled=True)  195 us
    all_to_all x1, waiting for transfers between devices, on_device(): lax.all_to_all(spectrum, 'band', split_axis=2, concat_axis=1, tiled=True)  148 us
    slice x2, local copies, waits for them, and re-layouts, on_device(): grad_band[1]  86.9 us
    transpose x1, local copies, waits for them, and re-layouts, on_device(): tile_view.transpose(0, 3, 1, 4, 2).reshape(2, tile_total, TILE, TILE)  84.8 us
    another operation x2, local copies, waits for them, and re-layouts, on_device(): model_grid = jnp.stack([grid_real, grid_imag]).astype(jnp.bfloat16)  81.6 us
    convert_element_type x1, other arithmetic, on_device(): grad_band.transpose(0, 2, 4, 1, 3).reshape(2, band_cols, side_cells)  63.8 us
    another operation x4, local copies, waits for them, and re-layouts, on_device(): jnp.stack([back_real, back_imag]).astype(jnp.bfloat16).transpose(0, 2, 1)  52.4 us
  transfers between devices with their start and end apart: 4, of which 3 were waited for; matrix products, arithmetic and copies ran while one was open for 8% of the time, Pallas kernels for 0%

commit v1 on v0

v1 whole, which is shorter than its diff:
```python
import math

import jax
import jax.numpy as jnp
import numpy as np
from jax import lax
from jax.experimental import pallas as pl
from jax.experimental.pallas import tpu as pltpu
from jax.sharding import PartitionSpec as P

RADIX = 128
SIDE = RADIX * RADIX
TILE = 64
HALF_BLOCKS = RADIX // 2
TILE_ROWS = SIDE // TILE
VIS_SLOT = 128
ROW_ALIGN = 16
ROWS_STEP = 16
STEP_PAIRS = 4
STEP_SLOTS = 2 * STEP_PAIRS
F32 = jnp.float32
BF16 = jnp.bfloat16
NT = (((1,), (1,)), ((), ()))
MIB = 1 << 20


def dot(a, b):
    return jnp.dot(a, b, preferred_element_type=F32)


def dot_nt(a, b):
    return lax.dot_general(a, b, NT, preferred_element_type=F32)


def radix_tables():
    index = np.arange(RADIX)
    angle = (index[:, None] * index[None, :] % RADIX) * (2.0 * math.pi / RADIX)
    turn = (index[:, None] * index[None, :]) * (2.0 * math.pi / SIDE)
    twist = np.concatenate([np.cos(turn), np.sin(turn)]) / RADIX
    return np.cos(angle), np.sin(angle), twist.astype(np.float32)


def whole(shape, space=pltpu.VMEM):
    return pl.BlockSpec(shape, lambda *_: (0,) * len(shape), memory_space=space)


def rows_forward_kernel(sky_ref, head_ref, twist_ref, tail_ref, out_ref, apart, done):
    for a in range(RADIX):
        apart[pl.ds(a, ROWS_STEP, stride=RADIX), :] = sky_ref[:, a * RADIX:(a + 1) * RADIX].astype(F32)

    def two_rows(i, _):
        first = apart[pl.ds(pl.multiple_of(2 * i * RADIX, RADIX), RADIX), :]
        second = apart[pl.ds(pl.multiple_of((2 * i + 1) * RADIX, RADIX), RADIX), :]
        mixed = dot(head_ref[...], jnp.concatenate([first, second], axis=1).astype(BF16))
        twist_cos, twist_sin = twist_ref[:RADIX], twist_ref[RADIX:]
        for side in range(2):
            part = slice(side * RADIX, (side + 1) * RADIX)
            by_cos, by_sin = mixed[:RADIX, part], mixed[RADIX:, part]
            middle_real = by_cos * twist_cos - by_sin * twist_sin
            middle_imag = -(by_cos * twist_sin + by_sin * twist_cos)
            middle = jnp.concatenate([middle_real, middle_imag], axis=1).astype(BF16)
            done[pl.ds(pl.multiple_of((2 * i + side) * RADIX, RADIX), RADIX), :] = dot_nt(tail_ref[...], middle)
        return 0

    lax.fori_loop(0, ROWS_STEP // 2, two_rows, 0, unroll=2)
    for j in range(HALF_BLOCKS):
        real = done[pl.ds(j, ROWS_STEP, stride=RADIX), :]
        imag = done[pl.ds(HALF_BLOCKS + j, ROWS_STEP, stride=RADIX), :]
        out_ref[j] = jnp.concatenate([real, imag], axis=1).astype(BF16)


def rows_forward(sky):
    rows = sky.shape[0]
    cos, sin, twist = radix_tables()
    head = jnp.asarray(np.concatenate([cos, sin]), BF16)
    tail = jnp.asarray(np.block([[cos[:HALF_BLOCKS], sin[:HALF_BLOCKS]], [-sin[:HALF_BLOCKS], cos[:HALF_BLOCKS]]]), BF16)
    return pl.pallas_call(
        rows_forward_kernel,
        grid=(rows // ROWS_STEP,),
        in_specs=[pl.BlockSpec((ROWS_STEP, SIDE), lambda i: (i, 0)), whole(head.shape), whole(twist.shape), whole(tail.shape)],
        out_specs=pl.BlockSpec((HALF_BLOCKS, ROWS_STEP, 2 * RADIX), lambda i: (0, i, 0)),
        out_shape=jax.ShapeDtypeStruct((HALF_BLOCKS, rows, 2 * RADIX), BF16),
        scratch_shapes=[pltpu.VMEM((ROWS_STEP * RADIX, RADIX), F32), pltpu.VMEM((ROWS_STEP * RADIX, RADIX), F32)],
        compiler_params=pltpu.CompilerParams(vmem_limit_bytes=24 * MIB),
        cost_estimate=pl.CostEstimate(flops=rows * RADIX * RADIX * 1024, bytes_accessed=rows * SIDE * 4, transcendentals=0),
        name="rows_forward",
    )(sky, head, jnp.asarray(twist), tail)


def rows_inverse_kernel(in_ref, head_ref, twist_ref, tail_ref, out_ref, apart, done):
    for j in range(HALF_BLOCKS):
        apart[pl.ds(j, ROWS_STEP, stride=HALF_BLOCKS), :] = in_ref[j, :, :RADIX].astype(F32)
        apart[pl.ds(ROWS_STEP * HALF_BLOCKS + j, ROWS_STEP, stride=HALF_BLOCKS), :] = in_ref[j, :, RADIX:].astype(F32)

    def one_row(y, _):
        real = apart[pl.ds(pl.multiple_of(y * HALF_BLOCKS, HALF_BLOCKS), HALF_BLOCKS), :]
        imag = apart[pl.ds(pl.multiple_of((ROWS_STEP + y) * HALF_BLOCKS, HALF_BLOCKS), HALF_BLOCKS), :]
        mixed = dot(head_ref[...], jnp.concatenate([real, imag], axis=1).astype(BF16))
        twist_cos, twist_sin = twist_ref[:RADIX], twist_ref[RADIX:]
        first_real = mixed[:RADIX, :RADIX] - mixed[RADIX:, RADIX:]
        first_imag = mixed[RADIX:, :RADIX] + mixed[:RADIX, RADIX:]
        middle_real = first_real * twist_cos - first_imag * twist_sin
        middle_imag = first_real * twist_sin + first_imag * twist_cos
        middle = jnp.concatenate([middle_real, middle_imag], axis=1).astype(BF16)
        done[pl.ds(pl.multiple_of(y * RADIX, RADIX), RADIX), :] = dot_nt(tail_ref[...], middle)
        return 0

    lax.fori_loop(0, ROWS_STEP, one_row, 0, unroll=4)
    for j in range(RADIX):
        out_ref[:, j * RADIX:(j + 1) * RADIX] = done[pl.ds(j, ROWS_STEP, stride=RADIX), :].astype(BF16)


def rows_inverse(columns):
    rows = columns.shape[1]
    cos, sin, twist = radix_tables()
    head = jnp.asarray(np.concatenate([cos[:, :HALF_BLOCKS], sin[:, :HALF_BLOCKS]]), BF16)
    tail = jnp.asarray(np.concatenate([cos, -sin], axis=1), BF16)
    return pl.pallas_call(
        rows_inverse_kernel,
        grid=(rows // ROWS_STEP,),
        in_specs=[pl.BlockSpec((HALF_BLOCKS, ROWS_STEP, 2 * RADIX), lambda i: (0, i, 0)), whole(head.shape), whole(twist.shape), whole(tail.shape)],
        out_specs=pl.BlockSpec((ROWS_STEP, SIDE), lambda i: (i, 0)),
        out_shape=jax.ShapeDtypeStruct((rows, SIDE), BF16),
        scratch_shapes=[pltpu.VMEM((2 * ROWS_STEP * HALF_BLOCKS, RADIX), F32), pltpu.VMEM((ROWS_STEP * RADIX, RADIX), F32)],
        compiler_params=pltpu.CompilerParams(vmem_limit_bytes=24 * MIB),
        cost_estimate=pl.CostEstimate(flops=rows * RADIX * RADIX * 1024, bytes_accessed=rows * SIDE * 4, transcendentals=0),
        name="rows_inverse",
    )(columns, head, jnp.asarray(twist), tail)


def pack_kernel(place_ref, half_ref, last_ref, weights_ref, out_ref):
    lane = lax.broadcasted_iota(jnp.int32, (VIS_SLOT, 2 * TILE), 1)

    def put(slot):
        block = weights_ref[slot].astype(F32)
        swapped = pltpu.roll(block, TILE, 1)
        keep = (lane * 0 + half_ref[slot]) == 1
        start = pl.multiple_of(place_ref[slot], ROW_ALIGN)
        out_ref[pl.ds(start, VIS_SLOT), :] = jnp.where(keep, block, swapped).astype(BF16)

    def one(slot, _):
        @pl.when(slot != last_ref[0])
        def _():
            put(slot)
        return 0

    lax.fori_loop(0, weights_ref.shape[0], one, 0)
    put(last_ref[0])


def pack(place, half, last, weights, pack_rows):
    return pl.pallas_call(
        pack_kernel,
        in_specs=[pl.BlockSpec(memory_space=pltpu.SMEM)] * 3 + [pl.BlockSpec(memory_space=pltpu.VMEM)],
        out_specs=pl.BlockSpec(memory_space=pltpu.VMEM),
        out_shape=jax.ShapeDtypeStruct((pack_rows, 2 * TILE), BF16),
        compiler_params=pltpu.CompilerParams(vmem_limit_bytes=16 * MIB),
        cost_estimate=pl.CostEstimate(flops=0, bytes_accessed=4 * MIB, transcendentals=0),
        name="pack",
    )(place, half, last, weights)


def fetch(order_ref, start_ref, packed_ref, blocks, sems, step, buffer):
    copies = []
    for i in range(STEP_SLOTS):
        slot = order_ref[step * STEP_SLOTS + i]
        start = pl.multiple_of(start_ref[slot], ROW_ALIGN)
        copies.append(pltpu.make_async_copy(packed_ref.at[pl.ds(start, VIS_SLOT), :], blocks.at[buffer, i], sems.at[buffer, i]))
    return copies


def over_steps(order_ref, start_ref, steps, packed_ref, blocks, sems, work):
    for copy in fetch(order_ref, start_ref, packed_ref, blocks, sems, 0, 0):
        copy.start()

    def step_body(step, _):
        buffer = lax.rem(step, 2)

        @pl.when(step + 1 < steps)
        def _():
            for copy in fetch(order_ref, start_ref, packed_ref, blocks, sems, step + 1, 1 - buffer):
                copy.start()

        for copy in fetch(order_ref, start_ref, packed_ref, blocks, sems, step, buffer):
            copy.wait()
        work(step, buffer)
        return 0

    lax.fori_loop(0, steps, step_body, 0)


def model_kernel(order_ref, start_ref, row_ref, half_ref, block_ref, steps_ref, table_ref, spectrum_ref, pick_ref, packed_ref, out_ref, blocks, sems):
    lane = lax.broadcasted_iota(jnp.int32, (VIS_SLOT, 2 * TILE), 1) // TILE

    def work(step, buffer):
        for pair in range(STEP_PAIRS):
            slots = [order_ref[step * STEP_SLOTS + 2 * pair + i] for i in range(2)]
            columns = spectrum_ref[block_ref[step * STEP_PAIRS + pair]]
            tables = jnp.concatenate([table_ref[row_ref[slot]] for slot in slots], axis=0)
            turned = dot(tables, columns)
            for i, slot in enumerate(slots):
                base = 2 * TILE * i
                by_cos, by_sin = turned[base:base + TILE], turned[base + TILE:base + 2 * TILE]
                tile_real = by_cos[:, :RADIX] + by_sin[:, RADIX:]
                tile_imag = by_cos[:, RADIX:] - by_sin[:, :RADIX]
                tile = jnp.concatenate([tile_real, tile_imag], axis=0).astype(BF16)
                weights = blocks[buffer, 2 * pair + i].astype(F32)
                along_u = lane == half_ref[slot]
                weights_u = jnp.where(along_u, weights, 0.0).astype(BF16)
                weights_v = jnp.where(along_u, pltpu.roll(weights, TILE, 1), weights)
                product = dot_nt(weights_u, tile) * weights_v
                high = product.astype(BF16)
                low = (product - high.astype(F32)).astype(BF16)
                summed = dot_nt(pick_ref[...], jnp.concatenate([high, low], axis=1))
                out_ref[slot] = summed[:2]

    over_steps(order_ref, start_ref, steps_ref[0], packed_ref, blocks, sems, work)


def model_parts(scalars, table, spectrum, packed, slot_rows):
    pick = np.zeros((16, 4 * TILE), np.float32)
    pick[0, :TILE] = pick[0, 2 * TILE:3 * TILE] = 1.0
    pick[1, TILE:2 * TILE] = pick[1, 3 * TILE:] = 1.0
    return pl.pallas_call(
        model_kernel,
        in_specs=[pl.BlockSpec(memory_space=pltpu.SMEM)] * 6 + [pl.BlockSpec(memory_space=pltpu.VMEM)] * 3 + [pl.BlockSpec(memory_space=pl.ANY)],
        out_specs=pl.BlockSpec(memory_space=pltpu.VMEM),
        out_shape=jax.ShapeDtypeStruct((slot_rows, 2, VIS_SLOT), F32),
        scratch_shapes=[pltpu.VMEM((2, STEP_SLOTS, VIS_SLOT, 2 * TILE), BF16), pltpu.SemaphoreType.DMA((2, STEP_SLOTS))],
        compiler_params=pltpu.CompilerParams(vmem_limit_bytes=52 * MIB),
        cost_estimate=pl.CostEstimate(flops=slot_rows * RADIX ** 3 * 6, bytes_accessed=64 * MIB, transcendentals=0),
        name="model",
    )(*scalars, table, spectrum, jnp.asarray(pick, BF16), packed)


def gradient_kernel(order_ref, start_ref, row_ref, half_ref, block_ref, steps_ref, table_ref, residual_ref, turn_ref, packed_ref, out_ref, total, blocks, sems):
    lane = lax.broadcasted_iota(jnp.int32, (VIS_SLOT, 2 * TILE), 1) // TILE

    def clear(j, _):
        total[j] = jnp.zeros(total.shape[1:], F32)
        return 0

    lax.fori_loop(0, HALF_BLOCKS, clear, 0)

    def work(step, buffer):
        for pair in range(STEP_PAIRS):
            slots = [order_ref[step * STEP_SLOTS + 2 * pair + i] for i in range(2)]
            tiles = []
            for i, slot in enumerate(slots):
                weights = blocks[buffer, 2 * pair + i]
                half = half_ref[slot]
                weights_u = jnp.where(lane == half, weights.astype(F32), 0.0).astype(BF16)
                turned_v = dot_nt(turn_ref[half], weights)
                residual = residual_ref[slot]
                weighted = jnp.concatenate([turned_v[:TILE] * residual[0:1], turned_v[TILE:] * residual[1:2]], axis=0)
                tile = dot(weighted.astype(BF16), weights_u)
                real, imag = tile[:TILE], tile[TILE:]
                tiles.append(jnp.concatenate([real, imag], axis=1))
                tiles.append(jnp.concatenate([-imag, real], axis=1))
            both = jnp.concatenate(tiles, axis=0).astype(BF16)
            tables = jnp.concatenate([table_ref[row_ref[slot]] for slot in slots], axis=1)
            block = block_ref[step * STEP_PAIRS + pair]
            total[block] = total[block] + dot(tables, both)

    over_steps(order_ref, start_ref, steps_ref[0], packed_ref, blocks, sems, work)

    def round_off(j, _):
        out_ref[j] = total[j].astype(BF16)
        return 0

    lax.fori_loop(0, HALF_BLOCKS, round_off, 0)


def gradient_columns(scalars, table, residual, packed, rows):
    turn = np.zeros((2, 2 * TILE, 2 * TILE), np.float32)
    for a in range(TILE):
        turn[0, [a, TILE + a], TILE + a] = 1.0
        turn[1, [a, TILE + a], a] = 1.0
    return pl.pallas_call(
        gradient_kernel,
        in_specs=[pl.BlockSpec(memory_space=pltpu.SMEM)] * 6 + [pl.BlockSpec(memory_space=pltpu.VMEM)] * 3 + [pl.BlockSpec(memory_space=pl.ANY)],
        out_specs=pl.BlockSpec(memory_space=pltpu.VMEM),
        out_shape=jax.ShapeDtypeStruct((HALF_BLOCKS, rows, 2 * RADIX), BF16),
        scratch_shapes=[
            pltpu.VMEM((HALF_BLOCKS, rows, 2 * RADIX), F32),
            pltpu.VMEM((2, STEP_SLOTS, VIS_SLOT, 2 * TILE), BF16),
            pltpu.SemaphoreType.DMA((2, STEP_SLOTS)),
        ],
        compiler_params=pltpu.CompilerParams(vmem_limit_bytes=56 * MIB),
        cost_estimate=pl.CostEstimate(flops=residual.shape[0] * RADIX ** 3 * 6, bytes_accessed=64 * MIB, transcendentals=0),
        name="gradient",
    )(*scalars, table, residual, jnp.asarray(turn, BF16), packed)


def column_tables(first_row, rows):
    y = first_row + jnp.arange(rows, dtype=jnp.int32)
    r = jnp.arange(TILE_ROWS, dtype=jnp.int32)
    a = jnp.arange(TILE, dtype=jnp.int32)
    coarse = (r[:, None] * y[None, :] % TILE_ROWS).astype(F32) * (2.0 * math.pi / TILE_ROWS)
    fine = (a[:, None] * y[None, :] % SIDE).astype(F32) * (2.0 * math.pi / SIDE)
    coarse_cos, coarse_sin = jnp.cos(coarse), jnp.sin(coarse)
    fine_cos, fine_sin = jnp.cos(fine) / RADIX, jnp.sin(fine) / RADIX
    with_cos = jnp.concatenate([fine_cos, fine_sin])
    with_sin = jnp.concatenate([fine_sin, -fine_cos])
    forward = coarse_cos[:, None, :] * with_cos[None] - coarse_sin[:, None, :] * with_sin[None]
    inverse = coarse_cos[:, :, None] * with_cos.T[None] - coarse_sin[:, :, None] * with_sin.T[None]
    return forward.astype(BF16), inverse.astype(BF16)


def pack_places(counts):
    padded = (counts + ROW_ALIGN - 1) // ROW_ALIGN * ROW_ALIGN
    slot = jnp.arange(counts.shape[1], dtype=jnp.int32)
    last = jnp.argmax(counts, axis=1).astype(jnp.int32)
    is_last = slot[None, :] == last[:, None]
    ahead = (slot[None, None, :] < slot[None, :, None]) & ~is_last[:, None, :] | (is_last[:, :, None] & ~is_last[:, None, :])
    return jnp.sum(jnp.where(ahead, padded[:, None, :], 0), axis=2), last


def spread(values, band_count):
    return lax.all_to_all(jnp.broadcast_to(values[None], (band_count,) + values.shape), "band", 0, 0, tiled=True)


def on_device(sky_image, tile_band, tile_place, counts, kernel, observed):
    band_count = lax.axis_size("band")
    rows = sky_image.shape[0]
    slots_here = tile_place.shape[0]
    slots_all = band_count * slots_here
    tiles_across = sky_image.shape[1] // 2 // band_count // TILE
    live_here = slots_here // 2 * VIS_SLOT
    pack_rows = (live_here + (slots_here - 1) * (ROW_ALIGN - 1)) // ROW_ALIGN * ROW_ALIGN

    tile_row = tile_place // tiles_across
    tile_col = tile_band[:, 0] * tiles_across + tile_place % tiles_across
    place, last = pack_places(counts)
    packed = lax.all_gather(pack(place[0], tile_col % 2, last, kernel, pack_rows), "band", tiled=True)

    every = spread(jnp.stack([tile_row, tile_col, counts[0]]), band_count)
    all_row, all_col, all_counts = (every[:, i].reshape(slots_all) for i in range(3))
    all_place, _ = pack_places(every[:, 2])
    all_start = (all_place + pack_rows * jnp.arange(band_count, dtype=jnp.int32)[:, None]).reshape(slots_all)
    all_block = all_col // 2

    spectrum = rows_forward(sky_image)
    forward_table, inverse_table = column_tables(lax.axis_index("band").astype(jnp.int32) * rows, rows)

    slot = jnp.arange(slots_all, dtype=jnp.int32)
    block = jnp.arange(HALF_BLOCKS, dtype=jnp.int32)
    in_block = jnp.sum((all_block[:, None] == block[None, :]).astype(jnp.int32), axis=0)
    pairs_of = (in_block + 1) // 2
    pairs_to = jnp.sum(jnp.where(block[None, :] <= block[:, None], pairs_of[None, :], 0), axis=1)
    rank = jnp.sum(((all_block[:, None] == all_block[None, :]) & (slot[None, :] < slot[:, None])).astype(jnp.int32), axis=1)
    first_pair = jnp.sum(jnp.where(block[None, :] < all_block[:, None], pairs_of[None, :], 0), axis=1)
    position = 2 * first_pair + rank
    steps_most = (slots_all + HALF_BLOCKS + STEP_SLOTS - 1) // STEP_SLOTS
    positions = jnp.arange(steps_most * STEP_SLOTS, dtype=jnp.int32)
    order = slots_all + jnp.sum(jnp.where(position[None, :] == positions[:, None], slot[None, :] - slots_all, 0), axis=1)
    pair_block = jnp.sum((pairs_to[None, :] <= positions[:steps_most * STEP_PAIRS, None]).astype(jnp.int32), axis=1)
    pair_block = jnp.minimum(pair_block, HALF_BLOCKS - 1)
    steps = (pairs_to[-1:] + STEP_PAIRS - 1) // STEP_PAIRS

    def spare(values):
        return jnp.pad(values, (0, 8))

    scalars = (order, spare(all_start), spare(all_row), spare(all_col % 2), pair_block, steps)
    parts = model_parts(scalars, forward_table, spectrum, packed, slots_all + 8)[:slots_all]
    parts = parts.reshape(band_count, slots_here, 2, VIS_SLOT)
    model = jnp.sum(lax.all_to_all(parts, "band", 0, 0, tiled=True), axis=0)
    live = jnp.arange(VIS_SLOT, dtype=jnp.int32)[None, None, :] < counts[0][:, None, None]
    residual = jnp.where(live, observed.astype(F32) - model, 0.0)
    residual = spread(residual, band_count).reshape(slots_all, 2, VIS_SLOT)
    residual = jnp.pad(residual, ((0, 8), (0, 0), (0, 0)))
    columns = gradient_columns(scalars, inverse_table, residual, packed, rows)
    return rows_inverse(columns)


def solution(mesh):
    return jax.shard_map(
        on_device,
        mesh=mesh,
        in_specs=(
            P(("parts", "band"), None),
            P(("parts", "band"), None),
            P(("parts", "band")),
            P(("parts", "band"), None),
            P(("parts", "band"), None, None),
            P(("parts", "band"), None, None),
        ),
        out_specs=P(("parts", "band"), None),
        check_vma=False,
    )
```

time: 1900 us -> 677 us (0.36); the launches traced: 1870 us -> 674 us
  local copies, waits for them, and re-layouts: 756 us -> 20.5 us
  Pallas kernels: 0 us -> 533 us
  matrix products: 447 us -> 0 us
  blocking collectives: 195 us -> 0 us
  waiting for transfers between devices: 227 us -> 49.1 us
  other arithmetic: 185 us -> 38.4 us
  starting transfers between devices: 64 us -> 18.9 us
    pallas_call x0 -> x5, Pallas kernels: none -> 533 us  [the longest x1 206 us: gradient_columns(): pl.pallas_call(gradient_kernel, in_specs=[pl.BlockSpec(memory_space=pltpu...]
    dot_general x32 -> x0, matrix products: 447 us -> none  [contract(): jnp.einsum(pattern, table_part, data_part, preferred_element_type=jnp.flo...]
    another operation x15 -> x2, local copies, waits for them, and re-layouts: 286 us -> 0.14 us  [on_device(): every[:, i].reshape(slots_all)]
    all_to_all x4 -> x3, waiting for transfers between devices: 227 us -> 24.9 us  [the longest x1 22.9 us: on_device(): model = jnp.sum(lax.all_to_all(parts, 'band', 0, 0, tiled=True), axis=0)]
    all_to_all x1 -> x0, blocking collectives: 195 us -> none  [on_device(): lax.all_to_all(back_stack, 'band', split_axis=1, concat_axis=2, tiled=True)]
    slice x4 -> x2, local copies, waits for them, and re-layouts: 135 us -> 1.71 us  [the longest x1 1.04 us: on_device(): model_parts(scalars, forward_table, spectrum, packed, slots_all + 8)]
    transpose x1 -> x0, local copies, waits for them, and re-layouts: 84.8 us -> none  [on_device(): tile_view.transpose(0, 3, 1, 4, 2).reshape(2, tile_total, TILE, TILE)]
    transpose x2 -> x0, other arithmetic: 63.2 us -> none  [the longest x1 44.3 us: on_device(): tile_view.transpose(0, 3, 1, 4, 2).reshape(2, tile_total, TILE, TILE)]
  transfers between devices with their start and end apart: 4 -> 4, of which waited for: 3 -> 3; matrix products, arithmetic and copies ran while one was open for 8% -> 5% of each run, Pallas kernels for 0% -> 8%
where the time goes in v1:
time: 677 us; the launch traced here: 674 us
  Pallas kernels  533 us (79%)
  waiting for transfers between devices  49.1 us (7%)
  other arithmetic  38.4 us (6%)
  local copies, waits for them, and re-layouts  20.5 us (3%)
  starting transfers between devices  18.9 us (3%)
  between operations  14.4 us (2%)
    pallas_call x1, Pallas kernels, gradient_columns(): pl.pallas_call(gradient_kernel, in_specs=[pl.BlockSpec(memory_space=pltpu...  206 us
    pallas_call x1, Pallas kernels, model_parts(): pl.pallas_call(model_kernel, in_specs=[pl.BlockSpec(memory_space=pltpu.SM...  175 us
    pallas_call x1, Pallas kernels, rows_inverse(): pl.pallas_call(rows_inverse_kernel, grid=(rows // ROWS_STEP,), in_specs=[...  91.8 us
    pallas_call x1, Pallas kernels, rows_forward(): pl.pallas_call(rows_forward_kernel, grid=(rows // ROWS_STEP,), in_specs=[...  52.7 us
    convert_element_type x2, other arithmetic, column_tables(): return (forward.astype(BF16), inverse.astype(BF16))  28.1 us
    all_gather x1, waiting for transfers between devices, on_device(): lax.all_gather(pack(place[0], tile_col % 2, last, kernel, pack_rows), 'ba...  24.1 us
    all_to_all x1, waiting for transfers between devices, on_device(): model = jnp.sum(lax.all_to_all(parts, 'band', 0, 0, tiled=True), axis=0)  22.9 us
    unnamed x38, local copies, waits for them, and re-layouts  15.2 us
  transfers between devices with their start and end apart: 4, of which 3 were waited for; matrix products, arithmetic and copies ran while one was open for 5% of the time, Pallas kernels for 8%

profile of v1, /device:TPU:0, one launch (start us, length us, event | category | flops | bytes accessed | tf_op | source)
XLA Modules:
  0.0 674.2 jit_solution(16342269307006674721)
XLA Ops:
  6.5 1.4 iota_reduce_fusion.1
  8.6 0.7 iota_compare_fusion.9
  9.3 0.7 and_select_fusion.1
  10.2 1.6 copy-done.3
  11.7 7.4 %pack.1 = bf16[5040,128]{1,0:T(8,128)(2,1)} custom-call(s32[64]{0:T(128)S(1)} %select_reduce_fusion.3.place_ref, s32[64]{0:T(128)S(1)} %get-tuple-element.11.half_ref, s32[1]{0:T(128)} %get-tuple-element.8.last_ref, bf16[64,128,128]{2,1,0:T(8,128)(2,1)S(1)} %copy-done.3), custom_call_target="tpu_custom_call" | custom-call | bytes 4194304 | tf_op jit(solution)/shard_map/pack/pallas_call | solution.py:152
  19.1 0.7 pad_add_fusion
  19.8 0.7 reshape.447
  20.5 7.4 %all-to-all-start = ((s32[16,1,192]{2,1,0:T(1,128)}), s32[16,1,192]{2,1,0:T(1,128)S(1)}, u32[]{:S(2)}, u32[]{:S(2)}) async-start(s32[16,1,192]{2,1,0:T(1,128)} %reshape.447), calls=%async_computation | async-start | bytes 32768 | tf_op jit(solution)/shard_map/all_to_all | solution.py:320
  28.9 1.0 fusion.13
  29.9 3.4 copy-done
  33.3 0.9 copy-done.4
  34.2 0.8 copy-done.8
  35.1 0.9 copy-done.9
  35.9 52.7 %rows_forward.1.spectrum_ref = bf16[64,256,256]{2,1,0:T(8,128)(2,1)S(1)} custom-call(bf16[256,16384]{1,0:T(8,128)(2,1)S(1)} %copy-done, bf16[256,128]{1,0:T(8,128)(2,1)S(1)} %copy-done.8, f32[256,128]{1,0:T(8,128)S(1)} %copy-done.4, bf16[128,256]{1,0:T(8,128)(2,1)S(1)} %copy-done.9), custom_call_target="tpu_custom_call" | custom-call | flops 4294967296 | bytes 16777216 | tf_op jit(solution)/shard_map/rows_forward/pallas_call | solution.py:77
  88.6 3.4 copy-done.1
  92.0 7.2 %subtract_convert_fusion.table_ref = bf16[256,128,256]{2,1,0:T(8,128)(2,1)} fusion(f32[128,256]{1,0:T(8,128)S(1)} %copy.20, f32[256,256]{1,0:T(8,128)S(1)} %get-tuple-element.20, f32[128,256]{1,0:T(8,128)S(1)} %copy.19, f32[256,256]{1,0:T(8,128)S(1)} %get-tuple-element.19), kind=kLoop, calls=%fused_computation | loop fusion | flops 33554432 | bytes 17563648 | tf_op jit(solution)/shard_map/convert_element_type | solution.py:307
  99.8 0.7 reduce.47
  101.1 0.7 slice.22
  102.5 0.7 iota_reduce_fusion
  105.4 24.1 %all-gather.2.cloned.1.call-done.packed_ref = bf16[80640,128]{1,0:T(8,128)(2,1)} async-done(((bf16[5040,128]{1,0:T(8,128)(2,1)}), bf16[80640,128]{1,0:T(8,128)(2,1)}) %all-gather.2.cloned.1.call-update) | async-done | bytes 20643856 | tf_op jit(solution)/shard_map/all_gather | solution.py:335
  129.6 174.8 %model.1 = f32[1032,2,128]{2,1,0:T(2,128)S(1)} custom-call(s32[1088]{0:T(1024)S(1)} %broadcast_add_fusion.1.order_ref, s32[1032]{0:T(1024)S(1)} %pad.14.start_ref, s32[1032]{0:T(1024)S(1)} %pad.15.row_ref, s32[1032]{0:T(1024)S(1)} %pad.16.half_ref, s32[544]{0:T(1024)S(1)} %broadcast_minimum_fusion.block_ref, s32[1]{0:T(128)S(6)} %select_n.134.steps_ref, ...), custom_call_target="tpu_custom_call" | custom-call | flops 12985565184 | bytes 67108864 | tf_op jit(solution)/shard_map/model/pallas_call | solution.py:224
  304.4 1.0 slice.27
  305.4 4.7 all-to-all-start.1
  310.2 22.9 %all-to-all-done.1 = f32[16,64,2,128]{3,2,1,0:T(2,128)S(1)} async-done(((f32[16,64,2,128]{3,2,1,0:T(2,128)}), f32[16,64,2,128]{3,2,1,0:T(2,128)S(1)}, u32[]{:S(2)}, u32[]{:S(2)}) %all-to-all-start.1) | async-done | bytes 1048608 | tf_op jit(solution)/shard_map/all_to_all | solution.py:367
  333.5 1.4 broadcast_in_dim.91
  334.9 6.9 %all-to-all-start.2 = ((f32[16,64,2,128]{3,2,1,0:T(2,128)}), f32[16,64,2,128]{3,2,1,0:T(2,128)S(1)}, u32[]{:S(2)}, u32[]{:S(2)}) async-start(f32[16,64,2,128]{3,2,1,0:T(2,128)} %broadcast_in_dim.91), calls=%async_computation.2 | async-start | bytes 2097152 | tf_op jit(solution)/shard_map/all_to_all | solution.py:320
  341.8 20.9 %subtract_convert_fusion.1.table_ref = bf16[256,256,128]{2,1,0:T(8,128)(2,1)} fusion(f32[256,128]{1,0:T(8,128)S(1)} %bitcast.18, f32[256,256]{1,0:T(8,128)S(1)} %get-tuple-element.20, f32[256,128]{1,0:T(8,128)S(1)} %bitcast.17, f32[256,256]{1,0:T(8,128)S(1)} %get-tuple-element.19), kind=kLoop, calls=%fused_computation.1 | loop fusion | flops 33554432 | bytes 17563648 | tf_op jit(solution)/shard_map/convert_element_type | solution.py:307
  362.6 2.1 all-to-all-done.2
  364.7 1.2 pad.17.residual_ref
  365.9 206.2 %gradient.1.in_ref = bf16[64,256,256]{2,1,0:T(8,128)(2,1)} custom-call(s32[1088]{0:T(1024)} %copy-done.13, s32[1032]{0:T(1024)} %copy-done.10, s32[1032]{0:T(1024)} %copy-done.12, s32[1032]{0:T(1024)} %copy-done.11, s32[544]{0:T(1024)} %copy-done.14, s32[1]{0:T(128)S(6)} %select_n.134.steps_ref, bf16[256,256,128]{2,1,0:T(8,128)(2,1)} %subtract_convert_fusion.1.table_ref, ...), custom_call_target="tpu_custom_call" | custom-call | flops 12985565184 | bytes 67108864 | tf_op jit(solution)/shard_map/gradient/pallas_call | solution.py:279
  572.2 3.4 copy-done.2
  575.5 91.8 %rows_inverse.1 = bf16[256,16384]{1,0:T(8,128)(2,1)} custom-call(bf16[64,256,256]{2,1,0:T(8,128)(2,1)S(1)} %copy-done.2, bf16[256,64]{1,0:T(8,128)(2,1)S(1)} %copy-done.6, f32[256,128]{1,0:T(8,128)S(1)} %copy-done.5, bf16[128,256]{1,0:T(8,128)(2,1)S(1)} %copy-done.7), custom_call_target="tpu_custom_call" | custom-call | flops 4294967296 | bytes 16777216 | tf_op jit(solution)/shard_map/rows_inverse/pallas_call | solution.py:118
  (69 shorter events, 5.6 us)
Async XLA Ops:
  6.5 123.0 %all-gather.2.cloned.1.call-start = ((), (), s32[]{:S(2)}) async-start(), calls=%async_computation.3 | async-start | bytes 21934080 | tf_op jit(solution)/shard_map/all_gather | solution.py:335
  10.1 1.6 copy-start.3
  20.5 78.7 %all-to-all-start = ((s32[16,1,192]{2,1,0:T(1,128)}), s32[16,1,192]{2,1,0:T(1,128)S(1)}, u32[]{:S(2)}, u32[]{:S(2)}) async-start(s32[16,1,192]{2,1,0:T(1,128)} %reshape.447), calls=%async_computation | async-start | bytes 32768 | tf_op jit(solution)/shard_map/all_to_all | solution.py:320
  29.9 3.4 copy-start
  33.3 0.9 copy-start.4
  34.2 0.8 copy-start.8
  35.0 0.9 copy-start.9
  35.9 93.6 %copy-start.15 = (bf16[16,256]{1,0:T(8,128)(2,1)S(1)}, bf16[16,256]{1,0:T(8,128)(2,1)}, u32[]{:S(2)}) copy-start(bf16[16,256]{1,0:T(8,128)(2,1)} %constant.204.clone.pick_ref) | copy-start | bytes 24580
  88.6 3.4 copy-start.1
  104.0 200.4 %copy-start.10 = (s32[1032]{0:T(1024)}, s32[1032]{0:T(1024)S(1)}, u32[]{:S(2)}) copy-start(s32[1032]{0:T(1024)S(1)} %pad.14.start_ref) | copy-start | bytes 12388
  104.0 200.4 %copy-start.11 = (s32[1032]{0:T(1024)}, s32[1032]{0:T(1024)S(1)}, u32[]{:S(2)}) copy-start(s32[1032]{0:T(1024)S(1)} %pad.16.half_ref) | copy-start | bytes 12388
  104.1 200.3 %copy-start.12 = (s32[1032]{0:T(1024)}, s32[1032]{0:T(1024)S(1)}, u32[]{:S(2)}) copy-start(s32[1032]{0:T(1024)S(1)} %pad.15.row_ref) | copy-start | bytes 12388
  105.4 199.0 %copy-start.14 = (s32[544]{0:T(1024)}, s32[544]{0:T(1024)S(1)}, u32[]{:S(2)}) copy-start(s32[544]{0:T(1024)S(1)} %broadcast_minimum_fusion.block_ref) | copy-start | bytes 6532
  105.4 199.0 %copy-start.13 = (s32[1088]{0:T(1024)}, s32[1088]{0:T(1024)S(1)}, u32[]{:S(2)}) copy-start(s32[1088]{0:T(1024)S(1)} %broadcast_add_fusion.1.order_ref) | copy-start | bytes 13060
  105.4 204.7 %copy-start.17 = (s32[1,64]{1,0:T(1,128)S(1)}, s32[1,64]{1,0:T(1,128)}, u32[]{:S(2)}) copy-start(s32[1,64]{1,0:T(1,128)} %param.17) | copy-start | bytes 772
  105.4 228.0 %copy-start.16 = (bf16[64,2,128]{2,1,0:T(2,128)(2,1)S(1)}, bf16[64,2,128]{2,1,0:T(2,128)(2,1)}, u32[]{:S(2)}) copy-start(bf16[64,2,128]{2,1,0:T(2,128)(2,1)} %param.19) | copy-start | bytes 98308
  305.4 27.6 %all-to-all-start.1 = ((f32[16,64,2,128]{3,2,1,0:T(2,128)}), f32[16,64,2,128]{3,2,1,0:T(2,128)S(1)}, u32[]{:S(2)}, u32[]{:S(2)}) async-start(f32[16,64,2,128]{3,2,1,0:T(2,128)} %bitcast.10), calls=%async_computation.1 | async-start | bytes 2097152 | tf_op jit(solution)/shard_map/all_to_all | solution.py:367
  334.9 29.8 %all-to-all-start.2 = ((f32[16,64,2,128]{3,2,1,0:T(2,128)}), f32[16,64,2,128]{3,2,1,0:T(2,128)S(1)}, u32[]{:S(2)}, u32[]{:S(2)}) async-start(f32[16,64,2,128]{3,2,1,0:T(2,128)} %broadcast_in_dim.91), calls=%async_computation.2 | async-start | bytes 2097152 | tf_op jit(solution)/shard_map/all_to_all | solution.py:320
  365.9 206.2 %copy-start.5 = (f32[256,128]{1,0:T(8,128)S(1)}, f32[256,128]{1,0:T(8,128)}, u32[]{:S(2)}) copy-start(f32[256,128]{1,0:T(8,128)} %constant.203.clone.twist_ref) | copy-start | bytes 393220
  365.9 206.2 %copy-start.6 = (bf16[256,64]{1,0:T(8,128)(2,1)S(1)}, bf16[256,64]{1,0:T(8,128)(2,1)}, u32[]{:S(2)}) copy-start(bf16[256,64]{1,0:T(8,128)(2,1)} %constant.206.clone.head_ref) | copy-start | bytes 98308
  365.9 206.2 %copy-start.7 = (bf16[128,256]{1,0:T(8,128)(2,1)S(1)}, bf16[128,256]{1,0:T(8,128)(2,1)}, u32[]{:S(2)}) copy-start(bf16[128,256]{1,0:T(8,128)(2,1)} %constant.207.clone.tail_ref) | copy-start | bytes 196612
  572.2 3.4 copy-start.2
Sparse Core Ops, SparseCore 0:
  19.3 110.2 all-gather.1

commit v2 on v1

v2 whole, which is shorter than its diff:
```python
import functools
import math

import jax
import jax.numpy as jnp
import numpy as np
from jax import lax
from jax.experimental import pallas as pl
from jax.experimental.pallas import tpu as pltpu
from jax.sharding import PartitionSpec as P

RADIX = 128
SIDE = RADIX * RADIX
TILE = 64
HALF_BLOCKS = RADIX // 2
TILE_ROWS = SIDE // TILE
VIS_SLOT = 128
ROW_PITCH = RADIX + 8
ROWS_STEP = 16
STEP_PAIRS = 8
STEP_SLOTS = 2 * STEP_PAIRS
BUFFERS = 4
TILES_PAIRS = 16
TILES_SLOTS = 2 * TILES_PAIRS
RESIDENT_BYTES = 16 << 20
F32 = jnp.float32
BF16 = jnp.bfloat16
NT = (((1,), (1,)), ((), ()))
MIB = 1 << 20


def dot(a, b):
    return jnp.dot(a, b, preferred_element_type=F32)


def dot_nt(a, b):
    return lax.dot_general(a, b, NT, preferred_element_type=F32)


def radix_tables():
    index = np.arange(RADIX)
    angle = (index[:, None] * index[None, :] % RADIX) * (2.0 * math.pi / RADIX)
    turn = (index[:, None] * index[None, :]) * (2.0 * math.pi / SIDE)
    twist = np.concatenate([np.cos(turn), np.sin(turn)]) / RADIX
    return np.cos(angle), np.sin(angle), twist.astype(np.float32)


def whole(shape, space=pltpu.VMEM):
    return pl.BlockSpec(shape, lambda *_: (0,) * len(shape), memory_space=space)


def two_by_two(apart, head_ref, tail_ref, done, twisted):
    def two_rows(i, _):
        first = apart[pl.ds(pl.multiple_of(2 * i * ROW_PITCH, 8), RADIX), :]
        second = apart[pl.ds(pl.multiple_of((2 * i + 1) * ROW_PITCH, 8), RADIX), :]
        mixed = dot(head_ref[...], jnp.concatenate([first, second], axis=1).astype(BF16))
        for side in range(2):
            part = slice(side * RADIX, (side + 1) * RADIX)
            middle = jnp.concatenate(twisted(mixed[:RADIX, part], mixed[RADIX:, part]), axis=1).astype(BF16)
            done[pl.ds(pl.multiple_of((2 * i + side) * ROW_PITCH, 8), RADIX), :] = dot_nt(tail_ref[...], middle)
        return 0

    lax.fori_loop(0, ROWS_STEP // 2, two_rows, 0, unroll=True)


def rows_forward_kernel(sky_ref, head_ref, twist_ref, tail_ref, out_ref, apart, done):
    for a in range(RADIX):
        apart[pl.ds(a, ROWS_STEP, stride=ROW_PITCH), :] = sky_ref[:, a * RADIX:(a + 1) * RADIX].astype(F32)

    def twisted(by_cos, by_sin):
        twist_cos, twist_sin = twist_ref[:RADIX], twist_ref[RADIX:]
        return [by_cos * twist_cos - by_sin * twist_sin, -(by_cos * twist_sin + by_sin * twist_cos)]

    two_by_two(apart, head_ref, tail_ref, done, twisted)
    for j in range(HALF_BLOCKS):
        real = done[pl.ds(j, ROWS_STEP, stride=ROW_PITCH), :]
        imag = done[pl.ds(HALF_BLOCKS + j, ROWS_STEP, stride=ROW_PITCH), :]
        out_ref[j] = jnp.concatenate([real, imag], axis=1).astype(BF16)


def rows_forward(sky):
    rows = sky.shape[0]
    cos, sin, twist = radix_tables()
    head = jnp.asarray(np.concatenate([cos, sin]), BF16)
    tail = jnp.asarray(np.block([[cos[:HALF_BLOCKS], sin[:HALF_BLOCKS]], [-sin[:HALF_BLOCKS], cos[:HALF_BLOCKS]]]), BF16)
    return pl.pallas_call(
        rows_forward_kernel,
        grid=(rows // ROWS_STEP,),
        in_specs=[pl.BlockSpec((ROWS_STEP, SIDE), lambda i: (i, 0)), whole(head.shape), whole(twist.shape), whole(tail.shape)],
        out_specs=pl.BlockSpec((HALF_BLOCKS, ROWS_STEP, 2 * RADIX), lambda i: (0, i, 0)),
        out_shape=jax.ShapeDtypeStruct((HALF_BLOCKS, rows, 2 * RADIX), BF16),
        scratch_shapes=[pltpu.VMEM((ROWS_STEP * ROW_PITCH, RADIX), F32), pltpu.VMEM((ROWS_STEP * ROW_PITCH, RADIX), F32)],
        compiler_params=pltpu.CompilerParams(vmem_limit_bytes=24 * MIB),
        cost_estimate=pl.CostEstimate(flops=rows * RADIX * RADIX * 1024, bytes_accessed=rows * SIDE * 4, transcendentals=0),
        name="rows_forward",
    )(sky, head, jnp.asarray(twist), tail)


def rows_inverse_kernel(in_ref, head_ref, twist_ref, tail_ref, out_ref, apart, done):
    for j in range(HALF_BLOCKS):
        apart[pl.ds(j, ROWS_STEP, stride=ROW_PITCH), :] = in_ref[j, :, :RADIX].astype(F32)
        apart[pl.ds(HALF_BLOCKS + j, ROWS_STEP, stride=ROW_PITCH), :] = in_ref[j, :, RADIX:].astype(F32)

    def twisted(real, imag):
        twist_cos, twist_sin = twist_ref[:RADIX], twist_ref[RADIX:]
        return [real * twist_cos - imag * twist_sin, real * twist_sin + imag * twist_cos]

    two_by_two(apart, head_ref, tail_ref, done, twisted)
    for j in range(RADIX):
        out_ref[:, j * RADIX:(j + 1) * RADIX] = done[pl.ds(j, ROWS_STEP, stride=ROW_PITCH), :].astype(BF16)


def rows_inverse(columns):
    rows = columns.shape[1]
    cos, sin, twist = radix_tables()
    used_cos, used_sin = cos[:, :HALF_BLOCKS], sin[:, :HALF_BLOCKS]
    head = jnp.asarray(np.block([[used_cos, -used_sin], [used_sin, used_cos]]), BF16)
    tail = jnp.asarray(np.concatenate([cos, -sin], axis=1), BF16)
    return pl.pallas_call(
        rows_inverse_kernel,
        grid=(rows // ROWS_STEP,),
        in_specs=[pl.BlockSpec((HALF_BLOCKS, ROWS_STEP, 2 * RADIX), lambda i: (0, i, 0)), whole(head.shape), whole(twist.shape), whole(tail.shape)],
        out_specs=pl.BlockSpec((ROWS_STEP, SIDE), lambda i: (i, 0)),
        out_shape=jax.ShapeDtypeStruct((rows, SIDE), BF16),
        scratch_shapes=[pltpu.VMEM((ROWS_STEP * ROW_PITCH, RADIX), F32), pltpu.VMEM((ROWS_STEP * ROW_PITCH, RADIX), F32)],
        compiler_params=pltpu.CompilerParams(vmem_limit_bytes=24 * MIB),
        cost_estimate=pl.CostEstimate(flops=rows * RADIX * RADIX * 1024, bytes_accessed=rows * SIDE * 4, transcendentals=0),
        name="rows_inverse",
    )(columns, head, jnp.asarray(twist), tail)


def pack_kernel(first_ref, weights_ref, observed_ref, out_ref, seen_ref, lined):
    column = lax.broadcasted_iota(jnp.int32, (8, VIS_SLOT), 1)

    def one(slot, _):
        first = first_ref[slot]
        lined[pl.ds(first, VIS_SLOT), :] = weights_ref[slot].astype(F32)
        tile, shift = first // VIS_SLOT, first % VIS_SLOT
        turned = pltpu.roll(observed_ref[slot], shift, 1)
        seen_ref[tile] = jnp.where(column >= shift, turned, seen_ref[tile])
        seen_ref[tile + 1] = turned
        return 0

    lax.fori_loop(0, weights_ref.shape[0], one, 0)
    for tile in range(out_ref.shape[0]):
        out_ref[tile] = lined[tile * VIS_SLOT:(tile + 1) * VIS_SLOT, :].T.astype(BF16)


def pack(first, weights, observed, tiles):
    return pl.pallas_call(
        pack_kernel,
        in_specs=[pl.BlockSpec(memory_space=pltpu.SMEM)] + [pl.BlockSpec(memory_space=pltpu.VMEM)] * 2,
        out_specs=[pl.BlockSpec(memory_space=pltpu.VMEM)] * 2,
        out_shape=[jax.ShapeDtypeStruct((tiles, 2 * TILE, VIS_SLOT), BF16), jax.ShapeDtypeStruct((tiles + 1, 8, VIS_SLOT), F32)],
        scratch_shapes=[pltpu.VMEM(((tiles + 1) * VIS_SLOT, 2 * TILE), F32)],
        compiler_params=pltpu.CompilerParams(vmem_limit_bytes=16 * MIB),
        cost_estimate=pl.CostEstimate(flops=0, bytes_accessed=4 * MIB, transcendentals=0),
        name="pack",
    )(first, weights, observed)


def tiles_kernel(order_ref, row_ref, block_ref, steps_ref, table_ref, spectrum_ref, out_ref, ready, sems):
    steps = (steps_ref[0] * STEP_PAIRS + TILES_PAIRS - 1) // TILES_PAIRS

    def leave(step, buffer):
        return pltpu.make_async_copy(ready.at[buffer], out_ref.at[pl.ds(step * TILES_SLOTS, TILES_SLOTS)], sems.at[buffer])

    def step_body(step, _):
        buffer = lax.rem(step, BUFFERS)

        @pl.when(step >= BUFFERS)
        def _():
            leave(step - BUFFERS, buffer).wait()

        for pair in range(TILES_PAIRS):
            slots = [order_ref[step * TILES_SLOTS + 2 * pair + i] for i in range(2)]
            columns = spectrum_ref[block_ref[step * TILES_PAIRS + pair]]
            tables = jnp.concatenate([table_ref[row_ref[slot]] for slot in slots], axis=0)
            turned = dot(tables, columns)
            for i in range(2):
                base = 2 * TILE * i
                by_cos, by_sin = turned[base:base + TILE], turned[base + TILE:base + 2 * TILE]
                ready[buffer, 2 * pair + i, :TILE] = (by_cos[:, :RADIX] + by_sin[:, RADIX:]).astype(BF16)
                ready[buffer, 2 * pair + i, TILE:] = (by_cos[:, RADIX:] - by_sin[:, :RADIX]).astype(BF16)
        leave(step, buffer).start()
        return 0

    lax.fori_loop(0, steps, step_body, 0)
    for back in range(BUFFERS, 0, -1):
        leave(steps - back, lax.rem(steps - back, BUFFERS)).wait()


def tile_parts(scalars, table, spectrum):
    order, window, low, high, row, half, block, steps = scalars
    return pl.pallas_call(
        tiles_kernel,
        in_specs=[pl.BlockSpec(memory_space=pltpu.SMEM)] * 4 + [pl.BlockSpec(memory_space=pltpu.VMEM)] * 2,
        out_specs=pl.BlockSpec(memory_space=pl.ANY),
        out_shape=jax.ShapeDtypeStruct((order.shape[0], 2 * TILE, RADIX), BF16),
        scratch_shapes=[pltpu.VMEM((BUFFERS, TILES_SLOTS, 2 * TILE, RADIX), BF16), pltpu.SemaphoreType.DMA((BUFFERS,))],
        compiler_params=pltpu.CompilerParams(vmem_limit_bytes=36 * MIB),
        cost_estimate=pl.CostEstimate(flops=order.shape[0] * RADIX ** 3 * 8, bytes_accessed=64 * MIB, transcendentals=0),
        name="tiles",
    )(order, row, block, steps, table, spectrum)


def copies(scalars, packed_ref, v_ref, u_ref, sems, step, buffer):
    order_ref, window_ref, half_ref = scalars
    started = []
    for i in range(STEP_SLOTS):
        slot = order_ref[step * STEP_SLOTS + i]
        window = window_ref[slot]
        half = half_ref[slot]
        from_row = pl.multiple_of(half * TILE, TILE)
        started.append(pltpu.make_async_copy(packed_ref.at[pl.ds(window, 2), :TILE], v_ref.at[buffer, i], sems.at[buffer, i, 0]))
        started.append(pltpu.make_async_copy(packed_ref.at[pl.ds(window, 2), TILE:], u_ref.at[buffer, i, half, :, pl.ds(from_row, TILE)], sems.at[buffer, i, 1]))
    return started


def over_steps(steps, fetch, work):
    ahead = BUFFERS - 1
    for step in range(ahead):
        for copy in fetch(step, step):
            copy.start()

    def step_body(step, _):
        buffer = lax.rem(step, BUFFERS)

        @pl.when(step + ahead < steps)
        def _():
            for copy in fetch(step + ahead, lax.rem(step + ahead, BUFFERS)):
                copy.start()

        for copy in fetch(step, buffer):
            copy.wait()
        work(step, buffer)
        return 0

    lax.fori_loop(0, steps, step_body, 0)


def clear_sides(u_ref):
    for buffer in range(BUFFERS):
        for i in range(STEP_SLOTS):
            u_ref[buffer, i] = jnp.zeros(u_ref.shape[2:], BF16)


def side_by_side(pair):
    return jnp.concatenate([pair[0], pair[1]], axis=1)


def model_kernel(resident, order_ref, window_ref, low_ref, high_ref, half_ref, steps_ref, packed_ref, tiles_ref, out_ref, t_ref, t_sems, *buffers):
    column = lax.broadcasted_iota(jnp.int32, (1, 2 * VIS_SLOT), 1)
    if not resident:
        v_ref, u_ref, sems = buffers
        clear_sides(u_ref)

    def fetch(step, buffer):
        started = [pltpu.make_async_copy(tiles_ref.at[pl.ds(step * STEP_SLOTS, STEP_SLOTS)], t_ref.at[buffer], t_sems.at[buffer])]
        if not resident:
            started += copies((order_ref, window_ref, half_ref), packed_ref, v_ref, u_ref, sems, step, buffer)
        return started

    def weights(i, slot, buffer):
        if not resident:
            return side_by_side(v_ref[buffer, i]), side_by_side(u_ref[buffer, i, half_ref[slot]])
        window = window_ref[slot]
        along_v = side_by_side([packed_ref[window, :TILE], packed_ref[window + 1, :TILE]])
        along_u = side_by_side([packed_ref[window, TILE:], packed_ref[window + 1, TILE:]])
        none = jnp.zeros_like(along_u)
        upper = half_ref[slot] == 1
        return along_v, jnp.concatenate([jnp.where(upper, none, along_u), jnp.where(upper, along_u, none)], axis=0)

    def work(step, buffer):
        found = []
        for i in range(STEP_SLOTS):
            slot = order_ref[step * STEP_SLOTS + i]
            weights_v, weights_u = weights(i, slot, buffer)
            inner = dot(t_ref[buffer, i], weights_u)
            weights_v = weights_v.astype(F32)
            real = jnp.sum(inner[:TILE] * weights_v, axis=0, keepdims=True)
            imag = jnp.sum(inner[TILE:] * weights_v, axis=0, keepdims=True)
            mine = (column >= low_ref[slot]) & (column < high_ref[slot])
            found.append((window_ref[slot], mine, jnp.concatenate([real, imag], axis=0)))
        for window, mine, both in found:
            out_ref[window] = jnp.where(mine[:, :VIS_SLOT], both[:, :VIS_SLOT], out_ref[window])
            out_ref[window + 1] = jnp.where(mine[:, VIS_SLOT:], both[:, VIS_SLOT:], out_ref[window + 1])

    over_steps(steps_ref[0], fetch, work)


def slot_buffers():
    return [
        pltpu.VMEM((BUFFERS, STEP_SLOTS, 2, TILE, VIS_SLOT), BF16),
        pltpu.VMEM((BUFFERS, STEP_SLOTS, 2, 2, 2 * TILE, VIS_SLOT), BF16),
    ]


def model_parts(scalars, packed, tiles):
    order, window, low, high, row, half, block, steps = scalars
    resident = packed.size * 2 <= RESIDENT_BYTES
    buffers = [] if resident else slot_buffers() + [pltpu.SemaphoreType.DMA((BUFFERS, STEP_SLOTS, 2))]
    return pl.pallas_call(
        functools.partial(model_kernel, resident),
        in_specs=[pl.BlockSpec(memory_space=pltpu.SMEM)] * 6 + [pl.BlockSpec(memory_space=pltpu.VMEM if resident else pl.ANY), pl.BlockSpec(memory_space=pl.ANY)],
        out_specs=pl.BlockSpec(memory_space=pltpu.VMEM),
        out_shape=jax.ShapeDtypeStruct((packed.shape[0], 2, VIS_SLOT), F32),
        scratch_shapes=[pltpu.VMEM((BUFFERS, STEP_SLOTS, 2 * TILE, RADIX), BF16), pltpu.SemaphoreType.DMA((BUFFERS,))] + buffers,
        compiler_params=pltpu.CompilerParams(vmem_limit_bytes=40 * MIB),
        cost_estimate=pl.CostEstimate(flops=order.shape[0] * RADIX ** 3 * 4, bytes_accessed=96 * MIB, transcendentals=0),
        name="model",
    )(order, window, low, high, half, steps, packed, tiles)


def gradient_kernel(order_ref, window_ref, low_ref, high_ref, row_ref, half_ref, block_ref, steps_ref, table_ref, residual_ref, packed_ref, out_ref, total, v_ref, u_ref, sems):
    column = lax.broadcasted_iota(jnp.int32, (1, 2 * VIS_SLOT), 1)
    clear_sides(u_ref)

    def clear(j, _):
        total[j] = jnp.zeros(total.shape[1:], F32)
        return 0

    lax.fori_loop(0, HALF_BLOCKS, clear, 0)

    def fetch(step, buffer):
        return copies((order_ref, window_ref, half_ref), packed_ref, v_ref, u_ref, sems, step, buffer)

    def work(step, buffer):
        found = []
        for pair in range(STEP_PAIRS):
            slots = [order_ref[step * STEP_SLOTS + 2 * pair + i] for i in range(2)]
            tiles = []
            for i, slot in enumerate(slots):
                at = 2 * pair + i
                window = window_ref[slot]
                mine = (column >= low_ref[slot]) & (column < high_ref[slot])
                residual = side_by_side([residual_ref[window], residual_ref[window + 1]])
                residual = jnp.where(mine, residual, 0.0)
                weights_v = side_by_side(v_ref[buffer, at]).astype(F32)
                weighted = jnp.concatenate([weights_v * residual[0:1], weights_v * residual[1:2]], axis=0).astype(BF16)
                tile = dot_nt(weighted, side_by_side(u_ref[buffer, at, half_ref[slot]]))
                real, imag = tile[:TILE], tile[TILE:]
                tiles.append(jnp.concatenate([real, imag], axis=1))
                tiles.append(jnp.concatenate([-imag, real], axis=1))
            found.append((slots, jnp.concatenate(tiles, axis=0).astype(BF16)))
        for pair, (slots, both) in enumerate(found):
            tables = jnp.concatenate([table_ref[row_ref[slot]] for slot in slots], axis=1)
            block = block_ref[step * STEP_PAIRS + pair]
            total[block] = total[block] + dot(tables, both)

    over_steps(steps_ref[0], fetch, work)

    def round_off(j, _):
        out_ref[j] = total[j].astype(BF16)
        return 0

    lax.fori_loop(0, HALF_BLOCKS, round_off, 0)


def gradient_columns(scalars, table, residual, packed, rows):
    return pl.pallas_call(
        gradient_kernel,
        in_specs=[pl.BlockSpec(memory_space=pltpu.SMEM)] * 8 + [pl.BlockSpec(memory_space=pltpu.VMEM)] * 2 + [pl.BlockSpec(memory_space=pl.ANY)],
        out_specs=pl.BlockSpec(memory_space=pltpu.VMEM),
        out_shape=jax.ShapeDtypeStruct((HALF_BLOCKS, rows, 2 * RADIX), BF16),
        scratch_shapes=[pltpu.VMEM((HALF_BLOCKS, rows, 2 * RADIX), F32)] + slot_buffers() + [pltpu.SemaphoreType.DMA((BUFFERS, STEP_SLOTS, 2))],
        compiler_params=pltpu.CompilerParams(vmem_limit_bytes=56 * MIB),
        cost_estimate=pl.CostEstimate(flops=scalars[0].shape[0] * RADIX ** 3 * 8, bytes_accessed=96 * MIB, transcendentals=0),
        name="gradient",
    )(*scalars, table, residual, packed)


def column_tables(first_row, rows):
    y = first_row + jnp.arange(rows, dtype=jnp.int32)
    r = jnp.arange(TILE_ROWS, dtype=jnp.int32)
    a = jnp.arange(TILE, dtype=jnp.int32)
    coarse = (r[:, None] * y[None, :] % TILE_ROWS).astype(F32) * (2.0 * math.pi / TILE_ROWS)
    fine = (a[:, None] * y[None, :] % SIDE).astype(F32) * (2.0 * math.pi / SIDE)
    coarse_cos, coarse_sin = jnp.cos(coarse), jnp.sin(coarse)
    fine_cos, fine_sin = jnp.cos(fine) / RADIX, jnp.sin(fine) / RADIX
    with_cos = jnp.concatenate([fine_cos, fine_sin])
    with_sin = jnp.concatenate([fine_sin, -fine_cos])
    forward = coarse_cos[:, None, :] * with_cos[None] - coarse_sin[:, None, :] * with_sin[None]
    inverse = coarse_cos[:, :, None] * with_cos.T[None] - coarse_sin[:, :, None] * with_sin.T[None]
    return forward.astype(BF16), inverse.astype(BF16)


def firsts(counts):
    slot = jnp.arange(counts.shape[1], dtype=jnp.int32)
    ahead = slot[None, None, :] < slot[None, :, None]
    return jnp.sum(jnp.where(ahead, counts[:, None, :], 0), axis=2)


def spread(values, band_count):
    return lax.all_to_all(jnp.broadcast_to(values[None], (band_count,) + values.shape), "band", 0, 0, tiled=True)


def on_device(sky_image, tile_band, tile_place, counts, kernel, observed):
    band_count = lax.axis_size("band")
    rows = sky_image.shape[0]
    slots_here = tile_place.shape[0]
    slots_all = band_count * slots_here
    tiles_across = sky_image.shape[1] // 2 // band_count // TILE
    tiles_here = slots_here // 2

    tile_row = tile_place // tiles_across
    tile_col = tile_band[:, 0] * tiles_across + tile_place % tiles_across
    seen = jnp.pad(observed.astype(F32), ((0, 0), (0, 6), (0, 0)))
    packed, seen = pack(firsts(counts)[0], kernel, seen, tiles_here)
    seen = seen[:tiles_here, :2]
    packed = lax.all_gather(packed, "band", tiled=True)

    every = spread(jnp.stack([tile_row, tile_col, counts[0]]), band_count)
    all_row, all_col = (every[:, i].reshape(slots_all) for i in range(2))
    all_block = all_col // 2
    all_first = firsts(every[:, 2])
    all_window = jnp.minimum(all_first // VIS_SLOT, tiles_here - 2)
    all_low = all_first - all_window * VIS_SLOT
    all_high = (all_low + every[:, 2]).reshape(slots_all)
    all_low = all_low.reshape(slots_all)
    all_window = (all_window + tiles_here * jnp.arange(band_count, dtype=jnp.int32)[:, None]).reshape(slots_all)

    spectrum = rows_forward(sky_image)
    forward_table, inverse_table = column_tables(lax.axis_index("band").astype(jnp.int32) * rows, rows)

    slot = jnp.arange(slots_all, dtype=jnp.int32)
    block = jnp.arange(HALF_BLOCKS, dtype=jnp.int32)
    in_block = jnp.sum((all_block[:, None] == block[None, :]).astype(jnp.int32), axis=0)
    pairs_of = (in_block + 1) // 2
    pairs_to = jnp.sum(jnp.where(block[None, :] <= block[:, None], pairs_of[None, :], 0), axis=1)
    rank = jnp.sum(((all_block[:, None] == all_block[None, :]) & (slot[None, :] < slot[:, None])).astype(jnp.int32), axis=1)
    first_pair = jnp.sum(jnp.where(block[None, :] < all_block[:, None], pairs_of[None, :], 0), axis=1)
    position = 2 * first_pair + rank
    positions_most = (slots_all + HALF_BLOCKS + TILES_SLOTS - 1) // TILES_SLOTS * TILES_SLOTS
    positions = jnp.arange(positions_most, dtype=jnp.int32)
    order = slots_all + jnp.sum(jnp.where(position[None, :] == positions[:, None], slot[None, :] - slots_all, 0), axis=1)
    pair_block = jnp.sum((pairs_to[None, :] <= positions[:positions_most // 2, None]).astype(jnp.int32), axis=1)
    pair_block = jnp.minimum(pair_block, HALF_BLOCKS - 1)
    steps = (pairs_to[-1:] + STEP_PAIRS - 1) // STEP_PAIRS

    def spare(values):
        return jnp.pad(values, (0, 8))

    scalars = (order, spare(all_window), spare(all_low), spare(all_high), spare(all_row), spare(all_col % 2), pair_block, steps)
    tiles = tile_parts(scalars, forward_table, spectrum)
    parts = model_parts(scalars, packed, tiles).reshape(band_count, tiles_here, 2, VIS_SLOT)
    residual = seen - jnp.sum(lax.all_to_all(parts, "band", 0, 0, tiled=True), axis=0)
    residual = spread(residual, band_count).reshape(band_count * tiles_here, 2, VIS_SLOT)
    columns = gradient_columns(scalars, inverse_table, residual, packed, rows)
    return rows_inverse(columns)


def solution(mesh):
    return jax.shard_map(
        on_device,
        mesh=mesh,
        in_specs=(
            P(("parts", "band"), None),
            P(("parts", "band"), None),
            P(("parts", "band")),
            P(("parts", "band"), None),
            P(("parts", "band"), None, None),
            P(("parts", "band"), None, None),
        ),
        out_specs=P(("parts", "band"), None),
        check_vma=False,
    )
```

time: 677 us -> 334 us (0.49)
  Pallas kernels: 533 us -> 188 us
  blocking collectives: 0 us -> 17.1 us
  starting transfers between devices: 18.9 us -> 11.5 us
  waiting for transfers between devices: 49.1 us -> 42.1 us
    pallas_call x1, Pallas kernels: 206 us -> 74.8 us  [gradient_columns(): pl.pallas_call(gradient_kernel, in_specs=[pl.BlockSpec(memory_space=pltpu...]
    pallas_call x1 -> x2, Pallas kernels: 175 us -> 68.1 us  [the longest x1 37.3 us: model_parts(): pl.pallas_call(functools.partial(model_kernel, resident), in_specs=[pl.Bl...]
    pallas_call x1, Pallas kernels: 91.8 us -> 19.5 us  [rows_inverse(): pl.pallas_call(rows_inverse_kernel, grid=(rows // ROWS_STEP,), in_specs=[...]
    pallas_call x1, Pallas kernels: 52.7 us -> 18.4 us  [rows_forward(): pl.pallas_call(rows_forward_kernel, grid=(rows // ROWS_STEP,), in_specs=[...]
    all_to_all x1 -> x0, waiting for transfers between devices: 22.9 us -> none  [on_device(): model = jnp.sum(lax.all_to_all(parts, 'band', 0, 0, tiled=True), axis=0)]
    all_gather x1, waiting for transfers between devices: 24.1 us -> 42 us  [on_device(): packed = lax.all_gather(packed, 'band', tiled=True)]
    all_to_all x0 -> x1, blocking collectives: none -> 17.1 us  [on_device(): lax.all_to_all(parts, 'band', 0, 0, tiled=True)]
    unnamed x38 -> x40, local copies, waits for them, and re-layouts: 15.2 us -> 20.9 us
  transfers between devices with their start and end apart: 4 -> 3, of which waited for: 3 -> 1; matrix products, arithmetic and copies ran while one was open for 5% -> 11% of each run, Pallas kernels for 8% -> 15%
where the time goes in v2:
time: 334 us; the launch traced here: 332 us
  Pallas kernels  188 us (56%)
  waiting for transfers between devices  42.1 us (13%)
  other arithmetic  35.5 us (11%)
  local copies, waits for them, and re-layouts  23.9 us (7%)
  blocking collectives  17.1 us (5%)
  between operations  14.5 us (4%)
  starting transfers between devices  11.5 us (3%)
    pallas_call x1, Pallas kernels, gradient_columns(): pl.pallas_call(gradient_kernel, in_specs=[pl.BlockSpec(memory_space=pltpu...  74.8 us
    all_gather x1, waiting for transfers between devices, on_device(): packed = lax.all_gather(packed, 'band', tiled=True)  42 us
    pallas_call x1, Pallas kernels, model_parts(): pl.pallas_call(functools.partial(model_kernel, resident), in_specs=[pl.Bl...  37.3 us
    pallas_call x1, Pallas kernels, tile_parts(): pl.pallas_call(tiles_kernel, in_specs=[pl.BlockSpec(memory_space=pltpu.SM...  30.8 us
    convert_element_type x2, other arithmetic, column_tables(): return (forward.astype(BF16), inverse.astype(BF16))  28 us
    unnamed x40, local copies, waits for them, and re-layouts  20.9 us
    pallas_call x1, Pallas kernels, rows_inverse(): pl.pallas_call(rows_inverse_kernel, grid=(rows // ROWS_STEP,), in_specs=[...  19.5 us
    pallas_call x1, Pallas kernels, rows_forward(): pl.pallas_call(rows_forward_kernel, grid=(rows // ROWS_STEP,), in_specs=[...  18.4 us
  transfers between devices with their start and end apart: 3, of which 1 were waited for; matrix products, arithmetic and copies ran while one was open for 11% of the time, Pallas kernels for 15%

profile of v2, /device:TPU:0, one launch (start us, length us, event | category | flops | bytes accessed | tf_op | source)
XLA Modules:
  0.0 332.1 jit_solution(17893376490690222563)
XLA Ops:
  6.5 0.8 pad_convert_fusion.observed_ref
  7.3 0.8 select_reduce_fusion.3.first_ref
  8.1 1.6 copy-done.4
  9.7 6.7 %pack.1 = (bf16[32,128,128]{2,1,0:T(8,128)(2,1)}, f32[33,8,128]{2,1,0:T(8,128)S(1)}) custom-call(s32[64]{0:T(128)S(1)} %select_reduce_fusion.3.first_ref, bf16[64,128,128]{2,1,0:T(8,128)(2,1)S(1)} %copy-done.4, f32[64,8,128]{2,1,0:T(8,128)S(1)} %pad_convert_fusion.observed_ref), custom_call_target="tpu_custom_call" | custom-call | bytes 4194304 | tf_op jit(solution)/shard_map/pack/pallas_call | solution.py:150
  16.4 0.7 fusion.24
  17.1 0.7 pad_add_fusion
  17.8 0.7 reshape.300
  18.5 7.4 %all-to-all-start = ((s32[16,1,192]{2,1,0:T(1,128)}), s32[16,1,192]{2,1,0:T(1,128)S(1)}, u32[]{:S(2)}, u32[]{:S(2)}) async-start(s32[16,1,192]{2,1,0:T(1,128)} %reshape.300), calls=%async_computation | async-start | bytes 32768 | tf_op jit(solution)/shard_map/all_to_all | solution.py:395
  25.9 0.6 cosine_multiply_fusion
  26.9 1.0 fusion.13
  27.9 3.7 %copy-done = bf16[256,16384]{1,0:T(8,128)(2,1)S(1)} copy-done((bf16[256,16384]{1,0:T(8,128)(2,1)S(1)}, bf16[256,16384]{1,0:T(8,128)(2,1)}, u32[]{:S(2)}) %copy-start) | copy-done | bytes 8388632
  31.6 0.9 copy-done.5
  32.5 0.8 copy-done.9
  33.4 0.8 copy-done.10
  34.2 18.4 %rows_forward.1.spectrum_ref = bf16[64,256,256]{2,1,0:T(8,128)(2,1)S(1)} custom-call(bf16[256,16384]{1,0:T(8,128)(2,1)S(1)} %copy-done, bf16[256,128]{1,0:T(8,128)(2,1)S(1)} %copy-done.9, f32[256,128]{1,0:T(8,128)S(1)} %copy-done.5, bf16[128,256]{1,0:T(8,128)(2,1)S(1)} %copy-done.10), custom_call_target="tpu_custom_call" | custom-call | flops 4294967296 | bytes 16777216 | tf_op jit(solution)/shard_map/rows_forward/pallas_call | solution.py:86
  52.7 3.4 %copy-done.1 = bf16[64,256,256]{2,1,0:T(8,128)(2,1)} copy-done((bf16[64,256,256]{2,1,0:T(8,128)(2,1)}, bf16[64,256,256]{2,1,0:T(8,128)(2,1)S(1)}, u32[]{:S(2)}) %copy-start.1) | copy-done | bytes 8388632
  56.0 7.2 %subtract_convert_fusion.table_ref = bf16[256,128,256]{2,1,0:T(8,128)(2,1)} fusion(f32[128,256]{1,0:T(8,128)S(1)} %copy.20, f32[256,256]{1,0:T(8,128)S(1)} %get-tuple-element.21, f32[128,256]{1,0:T(8,128)S(1)} %copy.19, f32[256,256]{1,0:T(8,128)S(1)} %get-tuple-element.20), kind=kLoop, calls=%fused_computation | loop fusion | flops 33554432 | bytes 17563648 | tf_op jit(solution)/shard_map/convert_element_type | solution.py:385
  63.4 0.6 broadcast.442
  64.0 0.7 reduce.13
  65.2 0.7 slice.23
  68.6 4.7 %copy-done.2 = bf16[64,256,256]{2,1,0:T(8,128)(2,1)S(1)} copy-done((bf16[64,256,256]{2,1,0:T(8,128)(2,1)S(1)}, bf16[64,256,256]{2,1,0:T(8,128)(2,1)}, u32[]{:S(2)}) %copy-start.2) | copy-done | bytes 8388632
  73.3 30.8 %tiles.1.tiles_ref = bf16[1088,128,128]{2,1,0:T(8,128)(2,1)} custom-call(s32[1088]{0:T(1024)S(1)} %broadcast_add_fusion.order_ref, s32[1032]{0:T(1024)S(1)} %pad.25.row_ref, s32[544]{0:T(1024)S(1)} %broadcast_minimum_fusion.block_ref, s32[1]{0:T(128)S(6)} %select_n.115.steps_ref, bf16[256,128,256]{2,1,0:T(8,128)(2,1)} %subtract_convert_fusion.table_ref, ...), custom_call_target="tpu_custom_call" | custom-call | flops 18253611008 | bytes 67108864 | tf_op jit(solution)/shard_map/tiles/pallas_call | solution.py:195
  104.1 42.0 %all-gather.2.cloned.1.call-done.packed_ref = bf16[512,128,128]{2,1,0:T(8,128)(2,1)} async-done(((bf16[32,128,128]{2,1,0:T(8,128)(2,1)}), bf16[512,128,128]{2,1,0:T(8,128)(2,1)}) %all-gather.2.cloned.1.call-update) | async-done | bytes 16777232 | tf_op jit(solution)/shard_map/all_gather | solution.py:411
  146.2 37.3 %model.1 = f32[512,2,128]{2,1,0:T(2,128)S(1)} custom-call(s32[1088]{0:T(1024)S(1)} %broadcast_add_fusion.order_ref, s32[1032]{0:T(1024)S(1)} %pad.22.window_ref, s32[1032]{0:T(1024)S(1)} %pad.23.low_ref, s32[1032]{0:T(1024)S(1)} %pad.24.high_ref, s32[1032]{0:T(1024)S(1)} %pad.26.half_ref, s32[1]{0:T(128)S(6)} %select_n.115.steps_ref, ...), custom_call_target="tpu_custom_call" | custom-call | flops 9126805504 | bytes 100663296 | tf_op jit(solution)/shard_map/model/pallas_call | solution.py:303
  183.4 17.1 %all_to_all.15 = f32[16,32,2,128]{3,2,1,0:T(2,128)S(1)} all-to-all(f32[16,32,2,128]{3,2,1,0:T(2,128)S(1)} %bitcast.14), channel_id=1, replica_groups=mesh['parts'=2,'band'=16] {'band'}, dimensions={0} | all-to-all | bytes 1048576 | tf_op jit(solution)/shard_map/all_to_all | solution.py:447
  200.8 1.0 broadcast_in_dim.133
  201.8 4.1 %all-to-all-start.2 = ((f32[16,32,2,128]{3,2,1,0:T(2,128)}), f32[16,32,2,128]{3,2,1,0:T(2,128)S(1)}, u32[]{:S(2)}, u32[]{:S(2)}) async-start(f32[16,32,2,128]{3,2,1,0:T(2,128)} %broadcast_in_dim.133), calls=%async_computation.2 | async-start | bytes 1048576 | tf_op jit(solution)/shard_map/all_to_all | solution.py:395
  205.9 20.8 %subtract_convert_fusion.1.table_ref = bf16[256,256,128]{2,1,0:T(8,128)(2,1)} fusion(f32[256,128]{1,0:T(8,128)S(1)} %bitcast.16, f32[256,256]{1,0:T(8,128)S(1)} %get-tuple-element.21, f32[256,128]{1,0:T(8,128)S(1)} %bitcast.15, f32[256,256]{1,0:T(8,128)S(1)} %get-tuple-element.20), kind=kLoop, calls=%fused_computation.1 | loop fusion | flops 33554432 | bytes 17563648 | tf_op jit(solution)/shard_map/convert_element_type | solution.py:385
  226.7 0.8 copy-done.18
  227.5 74.8 %gradient.1.in_ref = bf16[64,256,256]{2,1,0:T(8,128)(2,1)} custom-call(s32[1088]{0:T(1024)} %copy-done.15, s32[1032]{0:T(1024)} %copy-done.11, s32[1032]{0:T(1024)} %copy-done.12, s32[1032]{0:T(1024)} %copy-done.13, s32[1032]{0:T(1024)} %copy-done.16, s32[1032]{0:T(1024)} %copy-done.14, s32[544]{0:T(1024)} %copy-done.17, s32[1]{0:T(128)S(6)} %select_n.115.steps_ref, ...), custom_call_target="tpu_custom_call" | custom-call | flops 18253611008 | bytes 100663296 | tf_op jit(solution)/shard_map/gradient/pallas_call | solution.py:361
  302.3 3.4 %copy-done.3 = bf16[64,256,256]{2,1,0:T(8,128)(2,1)S(1)} copy-done((bf16[64,256,256]{2,1,0:T(8,128)(2,1)S(1)}, bf16[64,256,256]{2,1,0:T(8,128)(2,1)}, u32[]{:S(2)}) %copy-start.3) | copy-done | bytes 8388632
  305.7 19.5 %rows_inverse.1 = bf16[256,16384]{1,0:T(8,128)(2,1)} custom-call(bf16[64,256,256]{2,1,0:T(8,128)(2,1)S(1)} %copy-done.3, bf16[256,128]{1,0:T(8,128)(2,1)S(1)} %copy-done.7, f32[256,128]{1,0:T(8,128)S(1)} %copy-done.6, bf16[128,256]{1,0:T(8,128)(2,1)S(1)} %copy-done.8), custom_call_target="tpu_custom_call" | custom-call | flops 4294967296 | bytes 16777216 | tf_op jit(solution)/shard_map/rows_inverse/pallas_call | solution.py:119
  (69 shorter events, 3.1 us)
Async XLA Ops:
  6.5 139.6 %all-gather.2.cloned.1.call-start = ((), (), s32[]{:S(2)}) async-start(), calls=%async_computation.3 | async-start | bytes 17825792 | tf_op jit(solution)/shard_map/all_gather | solution.py:411
  8.1 1.6 copy-start.4
  18.5 44.9 %all-to-all-start = ((s32[16,1,192]{2,1,0:T(1,128)}), s32[16,1,192]{2,1,0:T(1,128)S(1)}, u32[]{:S(2)}, u32[]{:S(2)}) async-start(s32[16,1,192]{2,1,0:T(1,128)} %reshape.300), calls=%async_computation | async-start | bytes 32768 | tf_op jit(solution)/shard_map/all_to_all | solution.py:395
  27.9 3.7 %copy-start = (bf16[256,16384]{1,0:T(8,128)(2,1)S(1)}, bf16[256,16384]{1,0:T(8,128)(2,1)}, u32[]{:S(2)}) copy-start(bf16[256,16384]{1,0:T(8,128)(2,1)} %sky_ref.1) | copy-start | bytes 25165828
  31.6 0.9 copy-start.5
  32.5 0.8 copy-start.9
  33.4 0.8 copy-start.10
  52.6 3.4 %copy-start.1 = (bf16[64,256,256]{2,1,0:T(8,128)(2,1)}, bf16[64,256,256]{2,1,0:T(8,128)(2,1)S(1)}, u32[]{:S(2)}) copy-start(bf16[64,256,256]{2,1,0:T(8,128)(2,1)S(1)} %rows_forward.1.spectrum_ref) | copy-start | bytes 25165828
  66.7 37.4 %copy-start.16 = (s32[1032]{0:T(1024)}, s32[1032]{0:T(1024)S(1)}, u32[]{:S(2)}) copy-start(s32[1032]{0:T(1024)S(1)} %pad.25.row_ref) | copy-start | bytes 12388
  67.2 79.0 %copy-start.11 = (s32[1032]{0:T(1024)}, s32[1032]{0:T(1024)S(1)}, u32[]{:S(2)}) copy-start(s32[1032]{0:T(1024)S(1)} %pad.22.window_ref) | copy-start | bytes 12388
  67.2 78.9 %copy-start.12 = (s32[1032]{0:T(1024)}, s32[1032]{0:T(1024)S(1)}, u32[]{:S(2)}) copy-start(s32[1032]{0:T(1024)S(1)} %pad.23.low_ref) | copy-start | bytes 12388
  67.2 78.9 %copy-start.13 = (s32[1032]{0:T(1024)}, s32[1032]{0:T(1024)S(1)}, u32[]{:S(2)}) copy-start(s32[1032]{0:T(1024)S(1)} %pad.24.high_ref) | copy-start | bytes 12388
  67.2 78.9 %copy-start.14 = (s32[1032]{0:T(1024)}, s32[1032]{0:T(1024)S(1)}, u32[]{:S(2)}) copy-start(s32[1032]{0:T(1024)S(1)} %pad.26.half_ref) | copy-start | bytes 12388
  68.6 35.5 %copy-start.17 = (s32[544]{0:T(1024)}, s32[544]{0:T(1024)S(1)}, u32[]{:S(2)}) copy-start(s32[544]{0:T(1024)S(1)} %broadcast_minimum_fusion.block_ref) | copy-start | bytes 6532
  68.6 4.7 %copy-start.2 = (bf16[64,256,256]{2,1,0:T(8,128)(2,1)S(1)}, bf16[64,256,256]{2,1,0:T(8,128)(2,1)}, u32[]{:S(2)}) copy-start(bf16[64,256,256]{2,1,0:T(8,128)(2,1)} %copy-done.1) | copy-start | bytes 25165828
  73.3 72.9 %copy-start.15 = (s32[1088]{0:T(1024)}, s32[1088]{0:T(1024)S(1)}, u32[]{:S(2)}) copy-start(s32[1088]{0:T(1024)S(1)} %broadcast_add_fusion.order_ref) | copy-start | bytes 13060
  201.8 24.9 %all-to-all-start.2 = ((f32[16,32,2,128]{3,2,1,0:T(2,128)}), f32[16,32,2,128]{3,2,1,0:T(2,128)S(1)}, u32[]{:S(2)}, u32[]{:S(2)}) async-start(f32[16,32,2,128]{3,2,1,0:T(2,128)} %broadcast_in_dim.133), calls=%async_computation.2 | async-start | bytes 1048576 | tf_op jit(solution)/shard_map/all_to_all | solution.py:395
  226.7 0.8 copy-start.18
  227.5 74.8 %copy-start.6 = (f32[256,128]{1,0:T(8,128)S(1)}, f32[256,128]{1,0:T(8,128)}, u32[]{:S(2)}) copy-start(f32[256,128]{1,0:T(8,128)} %constant.170.clone.twist_ref) | copy-start | bytes 393220
  227.5 74.8 %copy-start.7 = (bf16[256,128]{1,0:T(8,128)(2,1)S(1)}, bf16[256,128]{1,0:T(8,128)(2,1)}, u32[]{:S(2)}) copy-start(bf16[256,128]{1,0:T(8,128)(2,1)} %constant.171.clone.head_ref) | copy-start | bytes 196612
  227.5 74.8 %copy-start.8 = (bf16[128,256]{1,0:T(8,128)(2,1)S(1)}, bf16[128,256]{1,0:T(8,128)(2,1)}, u32[]{:S(2)}) copy-start(bf16[128,256]{1,0:T(8,128)(2,1)} %constant.172.clone.tail_ref) | copy-start | bytes 196612
  302.3 3.4 %copy-start.3 = (bf16[64,256,256]{2,1,0:T(8,128)(2,1)S(1)}, bf16[64,256,256]{2,1,0:T(8,128)(2,1)}, u32[]{:S(2)}) copy-start(bf16[64,256,256]{2,1,0:T(8,128)(2,1)} %gradient.1.in_ref) | copy-start | bytes 25165828
Sparse Core Ops, SparseCore 0:
  16.6 129.5 all-gather.1

commit v3 on v2

--- a/solution.py
+++ b/solution.py
@@ -96,67 +96,93 @@
     )(sky, head, jnp.asarray(twist), tail)
 
 
-def rows_inverse_kernel(in_ref, head_ref, twist_ref, tail_ref, out_ref, apart, done):
-    for j in range(HALF_BLOCKS):
-        apart[pl.ds(j, ROWS_STEP, stride=ROW_PITCH), :] = in_ref[j, :, :RADIX].astype(F32)
-        apart[pl.ds(HALF_BLOCKS + j, ROWS_STEP, stride=ROW_PITCH), :] = in_ref[j, :, RADIX:].astype(F32)
+def rows_inverse(total, head_ref, twist_ref, tail_ref, out_ref, apart, done, lines, line_sems):
+    blocks = out_ref.shape[0] // ROWS_STEP
 
     def twisted(real, imag):
         twist_cos, twist_sin = twist_ref[:RADIX], twist_ref[RADIX:]
         return [real * twist_cos - imag * twist_sin, real * twist_sin + imag * twist_cos]
 
-    two_by_two(apart, head_ref, tail_ref, done, twisted)
-    for j in range(RADIX):
-        out_ref[:, j * RADIX:(j + 1) * RADIX] = done[pl.ds(j, ROWS_STEP, stride=ROW_PITCH), :].astype(BF16)
-
-
-def rows_inverse(columns):
-    rows = columns.shape[1]
+    def leave(i):
+        buffer = lax.rem(i, 2)
+        return pltpu.make_async_copy(lines.at[buffer], out_ref.at[pl.ds(pl.multiple_of(i * ROWS_STEP, ROWS_STEP), ROWS_STEP)], line_sems.at[buffer])
+
+    def one_block(i, _):
+        buffer = lax.rem(i, 2)
+        rows = pl.ds(pl.multiple_of(i * ROWS_STEP, ROWS_STEP), ROWS_STEP)
+        for j in range(HALF_BLOCKS):
+            apart[pl.ds(j, ROWS_STEP, stride=ROW_PITCH), :] = total[j, rows, :RADIX]
+            apart[pl.ds(HALF_BLOCKS + j, ROWS_STEP, stride=ROW_PITCH), :] = total[j, rows, RADIX:]
+        two_by_two(apart, head_ref, tail_ref, done, twisted)
+
+        @pl.when(i >= 2)
+        def _():
+            leave(i - 2).wait()
+
+        for j in range(RADIX):
+            lines[buffer, :, j * RADIX:(j + 1) * RADIX] = done[pl.ds(j, ROWS_STEP, stride=ROW_PITCH), :].astype(BF16)
+        leave(i).start()
+        return 0
+
+    lax.fori_loop(0, blocks, one_block, 0)
+    for back in range(min(2, blocks), 0, -1):
+        leave(blocks - back).wait()
+
+
+def inverse_tables():
     cos, sin, twist = radix_tables()
     used_cos, used_sin = cos[:, :HALF_BLOCKS], sin[:, :HALF_BLOCKS]
-    head = jnp.asarray(np.block([[used_cos, -used_sin], [used_sin, used_cos]]), BF16)
-    tail = jnp.asarray(np.concatenate([cos, -sin], axis=1), BF16)
-    return pl.pallas_call(
-        rows_inverse_kernel,
-        grid=(rows // ROWS_STEP,),
-        in_specs=[pl.BlockSpec((HALF_BLOCKS, ROWS_STEP, 2 * RADIX), lambda i: (0, i, 0)), whole(head.shape), whole(twist.shape), whole(tail.shape)],
-        out_specs=pl.BlockSpec((ROWS_STEP, SIDE), lambda i: (i, 0)),
-        out_shape=jax.ShapeDtypeStruct((rows, SIDE), BF16),
-        scratch_shapes=[pltpu.VMEM((ROWS_STEP * ROW_PITCH, RADIX), F32), pltpu.VMEM((ROWS_STEP * ROW_PITCH, RADIX), F32)],
-        compiler_params=pltpu.CompilerParams(vmem_limit_bytes=24 * MIB),
-        cost_estimate=pl.CostEstimate(flops=rows * RADIX * RADIX * 1024, bytes_accessed=rows * SIDE * 4, transcendentals=0),
-        name="rows_inverse",
-    )(columns, head, jnp.asarray(twist), tail)
-
-
-def pack_kernel(first_ref, weights_ref, observed_ref, out_ref, seen_ref, lined):
-    column = lax.broadcasted_iota(jnp.int32, (8, VIS_SLOT), 1)
-
+    head = np.block([[used_cos, -used_sin], [used_sin, used_cos]])
+    tail = np.concatenate([cos, -sin], axis=1)
+    return jnp.asarray(head, BF16), jnp.asarray(twist), jnp.asarray(tail, BF16)
+
+
+def pack_kernel(first_ref, weights_ref, out_ref, lined):
     def one(slot, _):
-        first = first_ref[slot]
-        lined[pl.ds(first, VIS_SLOT), :] = weights_ref[slot].astype(F32)
-        tile, shift = first // VIS_SLOT, first % VIS_SLOT
-        turned = pltpu.roll(observed_ref[slot], shift, 1)
-        seen_ref[tile] = jnp.where(column >= shift, turned, seen_ref[tile])
-        seen_ref[tile + 1] = turned
-        return 0
-
-    lax.fori_loop(0, weights_ref.shape[0], one, 0)
+        lined[pl.ds(first_ref[slot], VIS_SLOT), :] = weights_ref[slot].astype(F32)
+        return 0
+
+    lax.fori_loop(0, weights_ref.shape[0], one, 0, unroll=4)
     for tile in range(out_ref.shape[0]):
         out_ref[tile] = lined[tile * VIS_SLOT:(tile + 1) * VIS_SLOT, :].T.astype(BF16)
 
 
-def pack(first, weights, observed, tiles):
+def pack(first, weights, tiles):
     return pl.pallas_call(
         pack_kernel,
-        in_specs=[pl.BlockSpec(memory_space=pltpu.SMEM)] + [pl.BlockSpec(memory_space=pltpu.VMEM)] * 2,
-        out_specs=[pl.BlockSpec(memory_space=pltpu.VMEM)] * 2,
-        out_shape=[jax.ShapeDtypeStruct((tiles, 2 * TILE, VIS_SLOT), BF16), jax.ShapeDtypeStruct((tiles + 1, 8, VIS_SLOT), F32)],
+        in_specs=[pl.BlockSpec(memory_space=pltpu.SMEM), pl.BlockSpec(memory_space=pltpu.VMEM)],
+        out_specs=pl.BlockSpec(memory_space=pltpu.VMEM),
+        out_shape=jax.ShapeDtypeStruct((tiles, 2 * TILE, VIS_SLOT), BF16),
         scratch_shapes=[pltpu.VMEM(((tiles + 1) * VIS_SLOT, 2 * TILE), F32)],
         compiler_params=pltpu.CompilerParams(vmem_limit_bytes=16 * MIB),
         cost_estimate=pl.CostEstimate(flops=0, bytes_accessed=4 * MIB, transcendentals=0),
         name="pack",
-    )(first, weights, observed)
+    )(first, weights)
+
+
+def line_up_kernel(first_ref, observed_ref, seen_ref):
+    column = lax.broadcasted_iota(jnp.int32, (8, VIS_SLOT), 1)
+
+    def one(slot, _):
+        tile, shift = first_ref[slot] // VIS_SLOT, first_ref[slot] % VIS_SLOT
+        turned = pltpu.roll(observed_ref[slot], shift, 1)
+        seen_ref[tile] = jnp.where(column >= shift, turned, seen_ref[tile])
+        seen_ref[tile + 1] = turned
+        return 0
+
+    lax.fori_loop(0, observed_ref.shape[0], one, 0)
+
+
+def line_up(first, observed, tiles):
+    padded = jnp.pad(observed.astype(F32), ((0, 0), (0, 6), (0, 0)))
+    seen = pl.pallas_call(
+        line_up_kernel,
+        in_specs=[pl.BlockSpec(memory_space=pltpu.SMEM), pl.BlockSpec(memory_space=pltpu.VMEM)],
+        out_specs=pl.BlockSpec(memory_space=pltpu.VMEM),
+        out_shape=jax.ShapeDtypeStruct((tiles + 1, 8, VIS_SLOT), F32),
+        name="line_up",
+    )(first, padded)
+    return seen[:tiles, :2]
 
 
 def tiles_kernel(order_ref, row_ref, block_ref, steps_ref, table_ref, spectrum_ref, out_ref, ready, sems):
@@ -198,7 +224,7 @@
         out_specs=pl.BlockSpec(memory_space=pl.ANY),
         out_shape=jax.ShapeDtypeStruct((order.shape[0], 2 * TILE, RADIX), BF16),
         scratch_shapes=[pltpu.VMEM((BUFFERS, TILES_SLOTS, 2 * TILE, RADIX), BF16), pltpu.SemaphoreType.DMA((BUFFERS,))],
-        compiler_params=pltpu.CompilerParams(vmem_limit_bytes=36 * MIB),
+        compiler_params=pltpu.CompilerParams(vmem_limit_bytes=30 * MIB),
         cost_estimate=pl.CostEstimate(flops=order.shape[0] * RADIX ** 3 * 8, bytes_accessed=64 * MIB, transcendentals=0),
         name="tiles",
     )(order, row, block, steps, table, spectrum)
@@ -306,13 +332,13 @@
         out_specs=pl.BlockSpec(memory_space=pltpu.VMEM),
         out_shape=jax.ShapeDtypeStruct((packed.shape[0], 2, VIS_SLOT), F32),
         scratch_shapes=[pltpu.VMEM((BUFFERS, STEP_SLOTS, 2 * TILE, RADIX), BF16), pltpu.SemaphoreType.DMA((BUFFERS,))] + buffers,
-        compiler_params=pltpu.CompilerParams(vmem_limit_bytes=40 * MIB),
+        compiler_params=pltpu.CompilerParams(vmem_limit_bytes=22 * MIB),
         cost_estimate=pl.CostEstimate(flops=order.shape[0] * RADIX ** 3 * 4, bytes_accessed=96 * MIB, transcendentals=0),
         name="model",
     )(order, window, low, high, half, steps, packed, tiles)
 
 
-def gradient_kernel(order_ref, window_ref, low_ref, high_ref, row_ref, half_ref, block_ref, steps_ref, table_ref, residual_ref, packed_ref, out_ref, total, v_ref, u_ref, sems):
+def gradient_kernel(order_ref, window_ref, low_ref, high_ref, row_ref, half_ref, block_ref, steps_ref, table_ref, residual_ref, head_ref, twist_ref, tail_ref, packed_ref, out_ref, total, v_ref, u_ref, sems, *lines):
     column = lax.broadcasted_iota(jnp.int32, (1, 2 * VIS_SLOT), 1)
     clear_sides(u_ref)
 
@@ -350,24 +376,26 @@
 
     over_steps(steps_ref[0], fetch, work)
 
-    def round_off(j, _):
-        out_ref[j] = total[j].astype(BF16)
-        return 0
-
-    lax.fori_loop(0, HALF_BLOCKS, round_off, 0)
-
-
-def gradient_columns(scalars, table, residual, packed, rows):
+    rows_inverse(total, head_ref, twist_ref, tail_ref, out_ref, *lines)
+
+
+def gradient_rows(scalars, table, residual, packed, rows):
     return pl.pallas_call(
         gradient_kernel,
-        in_specs=[pl.BlockSpec(memory_space=pltpu.SMEM)] * 8 + [pl.BlockSpec(memory_space=pltpu.VMEM)] * 2 + [pl.BlockSpec(memory_space=pl.ANY)],
-        out_specs=pl.BlockSpec(memory_space=pltpu.VMEM),
-        out_shape=jax.ShapeDtypeStruct((HALF_BLOCKS, rows, 2 * RADIX), BF16),
-        scratch_shapes=[pltpu.VMEM((HALF_BLOCKS, rows, 2 * RADIX), F32)] + slot_buffers() + [pltpu.SemaphoreType.DMA((BUFFERS, STEP_SLOTS, 2))],
-        compiler_params=pltpu.CompilerParams(vmem_limit_bytes=56 * MIB),
+        in_specs=[pl.BlockSpec(memory_space=pltpu.SMEM)] * 8 + [pl.BlockSpec(memory_space=pltpu.VMEM)] * 5 + [pl.BlockSpec(memory_space=pl.ANY)],
+        out_specs=pl.BlockSpec(memory_space=pl.ANY),
+        out_shape=jax.ShapeDtypeStruct((rows, SIDE), BF16),
+        scratch_shapes=[pltpu.VMEM((HALF_BLOCKS, rows, 2 * RADIX), F32)] + slot_buffers() + [
+            pltpu.SemaphoreType.DMA((BUFFERS, STEP_SLOTS, 2)),
+            pltpu.VMEM((ROWS_STEP * ROW_PITCH, RADIX), F32),
+            pltpu.VMEM((ROWS_STEP * ROW_PITCH, RADIX), F32),
+            pltpu.VMEM((2, ROWS_STEP, SIDE), BF16),
+            pltpu.SemaphoreType.DMA((2,)),
+        ],
+        compiler_params=pltpu.CompilerParams(vmem_limit_bytes=47 * MIB),
         cost_estimate=pl.CostEstimate(flops=scalars[0].shape[0] * RADIX ** 3 * 8, bytes_accessed=96 * MIB, transcendentals=0),
         name="gradient",
-    )(*scalars, table, residual, packed)
+    )(*scalars, table, residual, *inverse_tables(), packed)
 
 
 def column_tables(first_row, rows):
@@ -382,7 +410,7 @@
     with_sin = jnp.concatenate([fine_sin, -fine_cos])
     forward = coarse_cos[:, None, :] * with_cos[None] - coarse_sin[:, None, :] * with_sin[None]
     inverse = coarse_cos[:, :, None] * with_cos.T[None] - coarse_sin[:, :, None] * with_sin.T[None]
-    return forward.astype(BF16), inverse.astype(BF16)
+    return lax.optimization_barrier((forward.astype(BF16), inverse.astype(BF16)))
 
 
 def firsts(counts):
@@ -405,10 +433,9 @@
 
     tile_row = tile_place // tiles_across
     tile_col = tile_band[:, 0] * tiles_across + tile_place % tiles_across
-    seen = jnp.pad(observed.astype(F32), ((0, 0), (0, 6), (0, 0)))
-    packed, seen = pack(firsts(counts)[0], kernel, seen, tiles_here)
-    seen = seen[:tiles_here, :2]
-    packed = lax.all_gather(packed, "band", tiled=True)
+    first = firsts(counts)[0]
+    packed = lax.all_gather(pack(first, kernel, tiles_here), "band", tiled=True)
+    seen = line_up(first, observed, tiles_here)
 
     every = spread(jnp.stack([tile_row, tile_col, counts[0]]), band_count)
     all_row, all_col = (every[:, i].reshape(slots_all) for i in range(2))
@@ -443,11 +470,11 @@
 
     scalars = (order, spare(all_window), spare(all_low), spare(all_high), spare(all_row), spare(all_col % 2), pair_block, steps)
     tiles = tile_parts(scalars, forward_table, spectrum)
-    parts = model_parts(scalars, packed, tiles).reshape(band_count, tiles_here, 2, VIS_SLOT)
-    residual = seen - jnp.sum(lax.all_to_all(parts, "band", 0, 0, tiled=True), axis=0)
-    residual = spread(residual, band_count).reshape(band_count * tiles_here, 2, VIS_SLOT)
-    columns = gradient_columns(scalars, inverse_table, residual, packed, rows)
-    return rows_inverse(columns)
+    parts = model_parts(scalars, packed, tiles).reshape(band_count, slots_here, VIS_SLOT)
+    model = jnp.sum(lax.all_to_all(parts.astype(BF16), "band", 0, 0, tiled=True).astype(F32), axis=0)
+    residual = seen.reshape(slots_here, VIS_SLOT) - model
+    residual = spread(residual.astype(BF16), band_count).astype(F32).reshape(band_count * tiles_here, 2, VIS_SLOT)
+    return gradient_rows(scalars, inverse_table, residual, packed, rows)
 
 
 def solution(mesh):

time: 334 us -> 306 us (0.916)
  waiting for transfers between devices: 42.1 us -> 27.4 us
  Pallas kernels: 188 us -> 183 us
  blocking collectives: 17.1 us -> 13.5 us
    all_gather x1, waiting for transfers between devices: 42 us -> 25.1 us  [on_device(): packed = lax.all_gather(pack(first, kernel, tiles_here), 'band', tiled=True)]
    pallas_call x1, Pallas kernels: 6.73 us -> 2.22 us  [pack(): pl.pallas_call(pack_kernel, in_specs=[pl.BlockSpec(memory_space=pltpu.SME...]
    pallas_call x1, Pallas kernels: 37.3 us -> 32.8 us  [model_parts(): pl.pallas_call(functools.partial(model_kernel, resident), in_specs=[pl.Bl...]
    all_to_all x2 -> x1, starting transfers between devices: 11.5 us -> 7.36 us  [spread(): lax.all_to_all(jnp.broadcast_to(values[None], (band_count,) + values.shap...]
    all_to_all x1, blocking collectives: 17.1 us -> 13.5 us  [spread(): lax.all_to_all(jnp.broadcast_to(values[None], (band_count,) + values.shap...]
    all_to_all x0 -> x1, starting transfers between devices: none -> 3.53 us  [on_device(): lax.all_to_all(parts.astype(BF16), 'band', 0, 0, tiled=True).astype(F32)]
    unnamed x40 -> x28, local copies, waits for them, and re-layouts: 20.9 us -> 17.9 us
    convert_element_type x2 -> x4, other arithmetic: 28 us -> 28.9 us  [the longest x1 20.8 us: column_tables(): inverse.astype(BF16)]
  transfers between devices with their start and end apart: 3 -> 3, of which waited for: 1 -> 2; matrix products, arithmetic and copies ran while one was open for 11% -> 12% of each run, Pallas kernels for 15% -> 18%
where the time goes in v3:
time: 306 us
  Pallas kernels  183 us (60%)
  other arithmetic  36.4 us (12%)
  waiting for transfers between devices  27.4 us (9%)
  local copies, waits for them, and re-layouts  20.8 us (7%)
  between operations  14.4 us (5%)
  blocking collectives  13.5 us (4%)
  starting transfers between devices  10.9 us (4%)
    pallas_call x1, Pallas kernels, gradient_rows(): pl.pallas_call(gradient_kernel, in_specs=[pl.BlockSpec(memory_space=pltpu...  91.4 us
    pallas_call x1, Pallas kernels, model_parts(): pl.pallas_call(functools.partial(model_kernel, resident), in_specs=[pl.Bl...  32.8 us
    pallas_call x1, Pallas kernels, tile_parts(): pl.pallas_call(tiles_kernel, in_specs=[pl.BlockSpec(memory_space=pltpu.SM...  31.5 us
    all_gather x1, waiting for transfers between devices, on_device(): packed = lax.all_gather(pack(first, kernel, tiles_here), 'band', tiled=True)  25.1 us
    convert_element_type x1, other arithmetic, column_tables(): inverse.astype(BF16)  20.8 us
    pallas_call x1, Pallas kernels, rows_forward(): pl.pallas_call(rows_forward_kernel, grid=(rows // ROWS_STEP,), in_specs=[...  18.6 us
    unnamed x28, local copies, waits for them, and re-layouts  17.9 us
    all_to_all x1, blocking collectives, spread(): lax.all_to_all(jnp.broadcast_to(values[None], (band_count,) + values.shap...  13.5 us
  transfers between devices with their start and end apart: 3, of which 2 were waited for; matrix products, arithmetic and copies ran while one was open for 12% of the time, Pallas kernels for 18%

profile of v3, /device:TPU:0, one launch (start us, length us, event | category | flops | bytes accessed | tf_op | source)
XLA Modules:
  0.0 306.0 jit_solution(18001120380085098078)
XLA Ops:
  6.5 0.8 select_reduce_fusion.3.first_ref
  7.3 1.6 copy-done.4
  8.9 2.2 pack.1
  11.2 0.7 fusion.24
  11.8 0.7 pad_add_fusion
  12.5 0.7 reshape.314
  13.2 7.4 %all-to-all-start = ((s32[16,1,192]{2,1,0:T(1,128)}), s32[16,1,192]{2,1,0:T(1,128)S(1)}, u32[]{:S(2)}, u32[]{:S(2)}) async-start(s32[16,1,192]{2,1,0:T(1,128)} %reshape.314), calls=%async_computation | async-start | bytes 32768 | tf_op jit(solution)/shard_map/all_to_all | solution.py:423
  20.6 0.6 cosine_multiply_fusion
  21.6 1.0 fusion.13
  22.6 3.7 %copy-done.1 = bf16[256,16384]{1,0:T(8,128)(2,1)S(1)} copy-done((bf16[256,16384]{1,0:T(8,128)(2,1)S(1)}, bf16[256,16384]{1,0:T(8,128)(2,1)}, u32[]{:S(2)}) %copy-start.1) | copy-done | bytes 8388632
  26.3 0.9 copy-done.5
  27.2 0.8 copy-done.7
  28.1 0.8 copy-done.8
  28.9 18.6 %rows_forward.1.spectrum_ref = bf16[64,256,256]{2,1,0:T(8,128)(2,1)S(1)} custom-call(bf16[256,16384]{1,0:T(8,128)(2,1)S(1)} %copy-done.1, bf16[256,128]{1,0:T(8,128)(2,1)S(1)} %copy-done.7, f32[256,128]{1,0:T(8,128)S(1)} %copy-done.5, bf16[128,256]{1,0:T(8,128)(2,1)S(1)} %copy-done.8), custom_call_target="tpu_custom_call" | custom-call | flops 4294967296 | bytes 16777216 | tf_op jit(solution)/shard_map/rows_forward/pallas_call | solution.py:86
  47.5 20.8 %subtract_convert_fusion.table_ref = bf16[256,256,128]{2,1,0:T(8,128)(2,1)} fusion(f32[256,128]{1,0:T(8,128)S(1)} %bitcast.17, f32[256,256]{1,0:T(8,128)S(1)} %get-tuple-element.21, f32[256,128]{1,0:T(8,128)S(1)} %bitcast.16, f32[256,256]{1,0:T(8,128)S(1)} %get-tuple-element.20), kind=kLoop, calls=%fused_computation | loop fusion | flops 33554432 | bytes 17563648 | tf_op jit(solution)/shard_map/convert_element_type | solution.py:413
  68.4 7.2 %subtract_convert_fusion.1.table_ref = bf16[256,128,256]{2,1,0:T(8,128)(2,1)} fusion(f32[128,256]{1,0:T(8,128)S(1)} %copy.20, f32[256,256]{1,0:T(8,128)S(1)} %get-tuple-element.21, f32[128,256]{1,0:T(8,128)S(1)} %copy.19, f32[256,256]{1,0:T(8,128)S(1)} %get-tuple-element.20), kind=kLoop, calls=%fused_computation.1 | loop fusion | flops 33554432 | bytes 17563648 | tf_op jit(solution)/shard_map/convert_element_type | solution.py:413
  75.7 0.6 broadcast.441
  76.3 0.7 reduce.13
  77.6 0.7 slice.23
  80.9 3.4 %copy-done.3 = bf16[64,256,256]{2,1,0:T(8,128)(2,1)S(1)} copy-done((bf16[64,256,256]{2,1,0:T(8,128)(2,1)S(1)}, bf16[64,256,256]{2,1,0:T(8,128)(2,1)}, u32[]{:S(2)}) %copy-start.3) | copy-done | bytes 8388632
  84.3 31.5 %tiles.1.tiles_ref = bf16[1088,128,128]{2,1,0:T(8,128)(2,1)} custom-call(s32[1088]{0:T(1024)S(1)} %broadcast_add_fusion.order_ref, s32[1032]{0:T(1024)S(1)} %pad.25.row_ref, s32[544]{0:T(1024)S(1)} %broadcast_minimum_fusion.block_ref, s32[1]{0:T(128)S(6)} %select_n.115.steps_ref, bf16[256,128,256]{2,1,0:T(8,128)(2,1)} %subtract_convert_fusion.1.table_ref, ...), custom_call_target="tpu_custom_call" | custom-call | flops 18253611008 | bytes 67108864 | tf_op jit(solution)/shard_map/tiles/pallas_call | solution.py:221
  115.8 25.1 %all-gather.2.cloned.1.call-done.packed_ref = bf16[512,128,128]{2,1,0:T(8,128)(2,1)} async-done(((bf16[32,128,128]{2,1,0:T(8,128)(2,1)}), bf16[512,128,128]{2,1,0:T(8,128)(2,1)}) %all-gather.2.cloned.1.call-update) | async-done | bytes 16777232 | tf_op jit(solution)/shard_map/all_gather | solution.py:437
  140.8 5.8 %copy-done = bf16[512,128,128]{2,1,0:T(8,128)(2,1)S(1)} copy-done((bf16[512,128,128]{2,1,0:T(8,128)(2,1)S(1)}, bf16[512,128,128]{2,1,0:T(8,128)(2,1)}, u32[]{:S(2)}) %copy-start) | copy-done | bytes 16777240
  146.6 32.8 %model.1 = f32[512,2,128]{2,1,0:T(2,128)S(1)} custom-call(s32[1088]{0:T(1024)S(1)} %broadcast_add_fusion.order_ref, s32[1032]{0:T(1024)S(1)} %pad.22.window_ref, s32[1032]{0:T(1024)S(1)} %pad.23.low_ref, s32[1032]{0:T(1024)S(1)} %pad.24.high_ref, s32[1032]{0:T(1024)S(1)} %pad.26.half_ref, s32[1]{0:T(128)S(6)} %select_n.115.steps_ref, ...), custom_call_target="tpu_custom_call" | custom-call | flops 9126805504 | bytes 100663296 | tf_op jit(solution)/shard_map/model/pallas_call | solution.py:329
  179.4 0.9 convert_element_type.62
  180.3 3.5 %all-to-all-start.1 = ((bf16[16,64,128]{2,1,0:T(8,128)(2,1)}), bf16[16,64,128]{2,1,0:T(8,128)(2,1)S(1)}, u32[]{:S(2)}, u32[]{:S(2)}) async-start(bf16[16,64,128]{2,1,0:T(8,128)(2,1)} %bitcast.8), calls=%async_computation.1 | async-start | bytes 524288 | tf_op jit(solution)/shard_map/all_to_all | solution.py:474
  183.8 0.7 pad_convert_fusion.observed_ref
  184.6 6.1 %line_up.1 = f32[33,8,128]{2,1,0:T(8,128)} custom-call(s32[64]{0:T(128)} %copy-done.9, f32[64,8,128]{2,1,0:T(8,128)} %pad_convert_fusion.observed_ref), custom_call_target="tpu_custom_call" | custom-call | tf_op jit(solution)/shard_map/line_up/pallas_call | solution.py:178
  190.6 0.9 slice.28
  191.6 2.3 all-to-all-done.1
  194.0 13.5 %all_to_all.15 = bf16[16,64,128]{2,1,0:T(8,128)(2,1)S(1)} all-to-all(bf16[16,64,128]{2,1,0:T(8,128)(2,1)S(1)} %broadcast_in_dim.133), channel_id=1, replica_groups=mesh['parts'=2,'band'=16] {'band'}, dimensions={0} | all-to-all | bytes 524288 | tf_op jit(solution)/shard_map/all_to_all | solution.py:423
  207.7 91.4 %gradient.1 = bf16[256,16384]{1,0:T(8,128)(2,1)} custom-call(s32[1088]{0:T(1024)S(1)} %broadcast_add_fusion.order_ref, s32[1032]{0:T(1024)S(1)} %pad.22.window_ref, s32[1032]{0:T(1024)S(1)} %pad.23.low_ref, s32[1032]{0:T(1024)S(1)} %pad.24.high_ref, s32[1032]{0:T(1024)S(1)} %pad.25.row_ref, s32[1032]{0:T(1024)S(1)} %pad.26.half_ref, ...), custom_call_target="tpu_custom_call" | custom-call | flops 18253611008 | bytes 100663296 | tf_op jit(solution)/shard_map/gradient/pallas_call | solution.py:383
  (60 shorter events, 3.2 us)
Async XLA Ops:
  6.5 134.3 %all-gather.2.cloned.1.call-start = ((), (), s32[]{:S(2)}) async-start(), calls=%async_computation.3 | async-start | bytes 17825792 | tf_op jit(solution)/shard_map/all_gather | solution.py:437
  7.3 1.6 copy-start.4
  8.9 59.5 %copy-start.9 = (s32[64]{0:T(128)}, s32[64]{0:T(128)S(1)}, u32[]{:S(2)}) copy-start(s32[64]{0:T(128)S(1)} %select_reduce_fusion.3.first_ref) | copy-start | bytes 772
  13.2 62.5 %all-to-all-start = ((s32[16,1,192]{2,1,0:T(1,128)}), s32[16,1,192]{2,1,0:T(1,128)S(1)}, u32[]{:S(2)}, u32[]{:S(2)}) async-start(s32[16,1,192]{2,1,0:T(1,128)} %reshape.314), calls=%async_computation | async-start | bytes 32768 | tf_op jit(solution)/shard_map/all_to_all | solution.py:423
  22.6 3.7 %copy-start.1 = (bf16[256,16384]{1,0:T(8,128)(2,1)S(1)}, bf16[256,16384]{1,0:T(8,128)(2,1)}, u32[]{:S(2)}) copy-start(bf16[256,16384]{1,0:T(8,128)(2,1)} %sky_ref.1) | copy-start | bytes 25165828
  26.3 0.9 copy-start.5
  27.2 0.8 copy-start.7
  28.1 0.8 copy-start.8
  47.5 28.1 %copy-start.2 = (bf16[64,256,256]{2,1,0:T(8,128)(2,1)}, bf16[64,256,256]{2,1,0:T(8,128)(2,1)S(1)}, u32[]{:S(2)}) copy-start(bf16[64,256,256]{2,1,0:T(8,128)(2,1)S(1)} %rows_forward.1.spectrum_ref) | copy-start | bytes 25165828
  80.9 3.4 %copy-start.3 = (bf16[64,256,256]{2,1,0:T(8,128)(2,1)S(1)}, bf16[64,256,256]{2,1,0:T(8,128)(2,1)}, u32[]{:S(2)}) copy-start(bf16[64,256,256]{2,1,0:T(8,128)(2,1)} %copy-done.2) | copy-start | bytes 25165828
  140.8 5.8 %copy-start = (bf16[512,128,128]{2,1,0:T(8,128)(2,1)S(1)}, bf16[512,128,128]{2,1,0:T(8,128)(2,1)}, u32[]{:S(2)}) copy-start(bf16[512,128,128]{2,1,0:T(8,128)(2,1)} %all-gather.2.cloned.1.call-done.packed_ref) | copy-start | bytes 50331652
  146.6 37.2 %copy-start.12 = (bf16[64,2,128]{2,1,0:T(2,128)(2,1)S(1)}, bf16[64,2,128]{2,1,0:T(2,128)(2,1)}, u32[]{:S(2)}) copy-start(bf16[64,2,128]{2,1,0:T(2,128)(2,1)} %param.17) | copy-start | bytes 98308
  146.6 61.1 %copy-start.6 = (f32[256,128]{1,0:T(8,128)S(1)}, f32[256,128]{1,0:T(8,128)}, u32[]{:S(2)}) copy-start(f32[256,128]{1,0:T(8,128)} %constant.170.clone.twist_ref) | copy-start | bytes 393220
  146.6 61.1 %copy-start.10 = (bf16[256,128]{1,0:T(8,128)(2,1)S(1)}, bf16[256,128]{1,0:T(8,128)(2,1)}, u32[]{:S(2)}) copy-start(bf16[256,128]{1,0:T(8,128)(2,1)} %constant.171.clone.head_ref) | copy-start | bytes 196612
  146.6 61.1 %copy-start.11 = (bf16[128,256]{1,0:T(8,128)(2,1)S(1)}, bf16[128,256]{1,0:T(8,128)(2,1)}, u32[]{:S(2)}) copy-start(bf16[128,256]{1,0:T(8,128)(2,1)} %constant.172.clone.tail_ref) | copy-start | bytes 196612
  180.3 13.5 %all-to-all-start.1 = ((bf16[16,64,128]{2,1,0:T(8,128)(2,1)}), bf16[16,64,128]{2,1,0:T(8,128)(2,1)S(1)}, u32[]{:S(2)}, u32[]{:S(2)}) async-start(bf16[16,64,128]{2,1,0:T(8,128)(2,1)} %bitcast.8), calls=%async_computation.1 | async-start | bytes 524288 | tf_op jit(solution)/shard_map/all_to_all | solution.py:474
Sparse Core Ops, SparseCore 0:
  11.3 129.5 all-gather.1

commit v4 on v3

--- a/solution.py
+++ b/solution.py
@@ -338,9 +338,9 @@
     )(order, window, low, high, half, steps, packed, tiles)
 
 
-def gradient_kernel(order_ref, window_ref, low_ref, high_ref, row_ref, half_ref, block_ref, steps_ref, table_ref, residual_ref, head_ref, twist_ref, tail_ref, packed_ref, out_ref, total, v_ref, u_ref, sems, *lines):
+def gradient_kernel(order_ref, window_ref, low_ref, high_ref, row_ref, half_ref, block_ref, steps_ref, table_ref, residual_ref, head_ref, twist_ref, tail_ref, packed_ref, out_ref, total, blocks_ref, sems, *lines):
     column = lax.broadcasted_iota(jnp.int32, (1, 2 * VIS_SLOT), 1)
-    clear_sides(u_ref)
+    sign = jnp.where(lax.broadcasted_iota(jnp.int32, (1, 2 * TILE), 1) < TILE, 1.0, -1.0)
 
     def clear(j, _):
         total[j] = jnp.zeros(total.shape[1:], F32)
@@ -349,7 +349,11 @@
     lax.fori_loop(0, HALF_BLOCKS, clear, 0)
 
     def fetch(step, buffer):
-        return copies((order_ref, window_ref, half_ref), packed_ref, v_ref, u_ref, sems, step, buffer)
+        started = []
+        for i in range(STEP_SLOTS):
+            window = window_ref[order_ref[step * STEP_SLOTS + i]]
+            started.append(pltpu.make_async_copy(packed_ref.at[pl.ds(window, 2)], blocks_ref.at[buffer, i], sems.at[buffer, i]))
+        return started
 
     def work(step, buffer):
         found = []
@@ -362,20 +366,24 @@
                 mine = (column >= low_ref[slot]) & (column < high_ref[slot])
                 residual = side_by_side([residual_ref[window], residual_ref[window + 1]])
                 residual = jnp.where(mine, residual, 0.0)
-                weights_v = side_by_side(v_ref[buffer, at]).astype(F32)
+                weights_v = side_by_side([blocks_ref[buffer, at, 0, :TILE], blocks_ref[buffer, at, 1, :TILE]]).astype(F32)
+                weights_u = side_by_side([blocks_ref[buffer, at, 0, TILE:], blocks_ref[buffer, at, 1, TILE:]])
                 weighted = jnp.concatenate([weights_v * residual[0:1], weights_v * residual[1:2]], axis=0).astype(BF16)
-                tile = dot_nt(weighted, side_by_side(u_ref[buffer, at, half_ref[slot]]))
-                real, imag = tile[:TILE], tile[TILE:]
-                tiles.append(jnp.concatenate([real, imag], axis=1))
-                tiles.append(jnp.concatenate([-imag, real], axis=1))
-            found.append((slots, jnp.concatenate(tiles, axis=0).astype(BF16)))
+                tile = dot_nt(weights_u, weighted)
+                real, imag = (tile * sign).astype(BF16), pltpu.roll(tile, TILE, 1).astype(BF16)
+                none = jnp.zeros_like(real)
+                upper = half_ref[slot] == 1
+                tiles.append(jnp.concatenate([
+                    jnp.where(upper, none, real), jnp.where(upper, real, none),
+                    jnp.where(upper, none, imag), jnp.where(upper, imag, none),
+                ], axis=0))
+            found.append((slots, jnp.concatenate(tiles, axis=1)))
         for pair, (slots, both) in enumerate(found):
             tables = jnp.concatenate([table_ref[row_ref[slot]] for slot in slots], axis=1)
             block = block_ref[step * STEP_PAIRS + pair]
-            total[block] = total[block] + dot(tables, both)
+            total[block] = total[block] + dot_nt(tables, both)
 
     over_steps(steps_ref[0], fetch, work)
-
     rows_inverse(total, head_ref, twist_ref, tail_ref, out_ref, *lines)
 
 
@@ -385,14 +393,15 @@
         in_specs=[pl.BlockSpec(memory_space=pltpu.SMEM)] * 8 + [pl.BlockSpec(memory_space=pltpu.VMEM)] * 5 + [pl.BlockSpec(memory_space=pl.ANY)],
         out_specs=pl.BlockSpec(memory_space=pl.ANY),
         out_shape=jax.ShapeDtypeStruct((rows, SIDE), BF16),
-        scratch_shapes=[pltpu.VMEM((HALF_BLOCKS, rows, 2 * RADIX), F32)] + slot_buffers() + [
-            pltpu.SemaphoreType.DMA((BUFFERS, STEP_SLOTS, 2)),
+        scratch_shapes=[pltpu.VMEM((HALF_BLOCKS, rows, 2 * RADIX), F32)] + [
+            pltpu.VMEM((BUFFERS, STEP_SLOTS, 2, 2 * TILE, VIS_SLOT), BF16),
+            pltpu.SemaphoreType.DMA((BUFFERS, STEP_SLOTS)),
             pltpu.VMEM((ROWS_STEP * ROW_PITCH, RADIX), F32),
             pltpu.VMEM((ROWS_STEP * ROW_PITCH, RADIX), F32),
             pltpu.VMEM((2, ROWS_STEP, SIDE), BF16),
             pltpu.SemaphoreType.DMA((2,)),
         ],
-        compiler_params=pltpu.CompilerParams(vmem_limit_bytes=47 * MIB),
+        compiler_params=pltpu.CompilerParams(vmem_limit_bytes=36 * MIB),
         cost_estimate=pl.CostEstimate(flops=scalars[0].shape[0] * RADIX ** 3 * 8, bytes_accessed=96 * MIB, transcendentals=0),
         name="gradient",
     )(*scalars, table, residual, *inverse_tables(), packed)

time: 306 us -> 310 us (1.013)
  local copies, waits for them, and re-layouts: 20.8 us -> 26.6 us
  Pallas kernels: 183 us -> 178 us
    unnamed x28 -> x30, local copies, waits for them, and re-layouts: 17.9 us -> 23.6 us
    pallas_call x1, Pallas kernels: 91.4 us -> 88.1 us  [gradient_rows(): pl.pallas_call(gradient_kernel, in_specs=[pl.BlockSpec(memory_space=pltpu...]
where the time goes in v4:
time: 310 us; the launch traced here: 308 us
  Pallas kernels  178 us (57%)
  other arithmetic  36.4 us (12%)
  waiting for transfers between devices  28.1 us (9%)
  local copies, waits for them, and re-layouts  26.6 us (9%)
  between operations  14.4 us (5%)
  blocking collectives  13.5 us (4%)
  starting transfers between devices  10.9 us (4%)
    pallas_call x1, Pallas kernels, gradient_rows(): pl.pallas_call(gradient_kernel, in_specs=[pl.BlockSpec(memory_space=pltpu...  88.1 us
    pallas_call x1, Pallas kernels, model_parts(): pl.pallas_call(functools.partial(model_kernel, resident), in_specs=[pl.Bl...  32.3 us
    pallas_call x1, Pallas kernels, tile_parts(): pl.pallas_call(tiles_kernel, in_specs=[pl.BlockSpec(memory_space=pltpu.SM...  30.7 us
    all_gather x1, waiting for transfers between devices, on_device(): packed = lax.all_gather(pack(first, kernel, tiles_here), 'band', tiled=True)  25.8 us
    unnamed x30, local copies, waits for them, and re-layouts  23.6 us
    convert_element_type x1, other arithmetic, column_tables(): inverse.astype(BF16)  20.8 us
    pallas_call x1, Pallas kernels, rows_forward(): pl.pallas_call(rows_forward_kernel, grid=(rows // ROWS_STEP,), in_specs=[...  18.6 us
    all_to_all x1, blocking collectives, spread(): lax.all_to_all(jnp.broadcast_to(values[None], (band_count,) + values.shap...  13.5 us
  transfers between devices with their start and end apart: 3, of which 2 were waited for; matrix products, arithmetic and copies ran while one was open for 12% of the time, Pallas kernels for 18%

profile of v4, /device:TPU:0, one launch (start us, length us, event | category | flops | bytes accessed | tf_op | source)
XLA Modules:
  0.0 307.9 jit_solution(1627225861047710713)
XLA Ops:
  6.5 0.8 select_reduce_fusion.3.first_ref
  7.3 1.6 copy-done.5
  8.9 2.2 pack.1
  11.2 0.7 fusion.24
  11.8 0.7 pad_add_fusion
  12.5 0.7 reshape.314
  13.2 7.4 %all-to-all-start = ((s32[16,1,192]{2,1,0:T(1,128)}), s32[16,1,192]{2,1,0:T(1,128)S(1)}, u32[]{:S(2)}, u32[]{:S(2)}) async-start(s32[16,1,192]{2,1,0:T(1,128)} %reshape.314), calls=%async_computation | async-start | bytes 32768 | tf_op jit(solution)/shard_map/all_to_all | solution.py:432
  20.6 0.6 cosine_multiply_fusion
  21.6 1.0 fusion.13
  22.6 3.7 %copy-done.2 = bf16[256,16384]{1,0:T(8,128)(2,1)S(1)} copy-done((bf16[256,16384]{1,0:T(8,128)(2,1)S(1)}, bf16[256,16384]{1,0:T(8,128)(2,1)}, u32[]{:S(2)}) %copy-start.2) | copy-done | bytes 8388632
  26.3 0.9 copy-done.6
  27.2 0.8 copy-done.8
  28.1 0.8 copy-done.9
  28.9 18.6 %rows_forward.1.spectrum_ref = bf16[64,256,256]{2,1,0:T(8,128)(2,1)S(1)} custom-call(bf16[256,16384]{1,0:T(8,128)(2,1)S(1)} %copy-done.2, bf16[256,128]{1,0:T(8,128)(2,1)S(1)} %copy-done.8, f32[256,128]{1,0:T(8,128)S(1)} %copy-done.6, bf16[128,256]{1,0:T(8,128)(2,1)S(1)} %copy-done.9), custom_call_target="tpu_custom_call" | custom-call | flops 4294967296 | bytes 16777216 | tf_op jit(solution)/shard_map/rows_forward/pallas_call | solution.py:86
  47.5 20.8 %subtract_convert_fusion.table_ref = bf16[256,256,128]{2,1,0:T(8,128)(2,1)} fusion(f32[256,128]{1,0:T(8,128)S(1)} %bitcast.17, f32[256,256]{1,0:T(8,128)S(1)} %get-tuple-element.21, f32[256,128]{1,0:T(8,128)S(1)} %bitcast.16, f32[256,256]{1,0:T(8,128)S(1)} %get-tuple-element.20), kind=kLoop, calls=%fused_computation | loop fusion | flops 33554432 | bytes 17563648 | tf_op jit(solution)/shard_map/convert_element_type | solution.py:422
  68.4 7.2 %subtract_convert_fusion.1.table_ref = bf16[256,128,256]{2,1,0:T(8,128)(2,1)} fusion(f32[128,256]{1,0:T(8,128)S(1)} %copy.20, f32[256,256]{1,0:T(8,128)S(1)} %get-tuple-element.21, f32[128,256]{1,0:T(8,128)S(1)} %copy.19, f32[256,256]{1,0:T(8,128)S(1)} %get-tuple-element.20), kind=kLoop, calls=%fused_computation.1 | loop fusion | flops 33554432 | bytes 17563648 | tf_op jit(solution)/shard_map/convert_element_type | solution.py:422
  76.3 0.7 reduce.13
  77.6 0.7 slice.23
  80.9 3.4 %copy-done.4 = bf16[64,256,256]{2,1,0:T(8,128)(2,1)S(1)} copy-done((bf16[64,256,256]{2,1,0:T(8,128)(2,1)S(1)}, bf16[64,256,256]{2,1,0:T(8,128)(2,1)}, u32[]{:S(2)}) %copy-start.4) | copy-done | bytes 8388632
  84.3 30.7 %tiles.1.tiles_ref = bf16[1088,128,128]{2,1,0:T(8,128)(2,1)} custom-call(s32[1088]{0:T(1024)S(1)} %broadcast_add_fusion.order_ref, s32[1032]{0:T(1024)S(1)} %pad.25.row_ref, s32[544]{0:T(1024)S(1)} %broadcast_minimum_fusion.block_ref, s32[1]{0:T(128)S(6)} %select_n.115.steps_ref, bf16[256,128,256]{2,1,0:T(8,128)(2,1)} %subtract_convert_fusion.1.table_ref, ...), custom_call_target="tpu_custom_call" | custom-call | flops 18253611008 | bytes 67108864 | tf_op jit(solution)/shard_map/tiles/pallas_call | solution.py:221
  115.0 25.8 %all-gather.2.cloned.1.call-done.packed_ref = bf16[512,128,128]{2,1,0:T(8,128)(2,1)} async-done(((bf16[32,128,128]{2,1,0:T(8,128)(2,1)}), bf16[512,128,128]{2,1,0:T(8,128)(2,1)}) %all-gather.2.cloned.1.call-update) | async-done | bytes 16777232 | tf_op jit(solution)/shard_map/all_gather | solution.py:446
  140.8 5.8 %copy-done.1 = bf16[512,128,128]{2,1,0:T(8,128)(2,1)S(1)} copy-done((bf16[512,128,128]{2,1,0:T(8,128)(2,1)S(1)}, bf16[512,128,128]{2,1,0:T(8,128)(2,1)}, u32[]{:S(2)}) %copy-start.1) | copy-done | bytes 16777240
  146.6 32.3 %model.1 = f32[512,2,128]{2,1,0:T(2,128)S(1)} custom-call(s32[1088]{0:T(1024)S(1)} %broadcast_add_fusion.order_ref, s32[1032]{0:T(1024)S(1)} %pad.22.window_ref, s32[1032]{0:T(1024)S(1)} %pad.23.low_ref, s32[1032]{0:T(1024)S(1)} %pad.24.high_ref, s32[1032]{0:T(1024)S(1)} %pad.26.half_ref, s32[1]{0:T(128)S(6)} %select_n.115.steps_ref, ...), custom_call_target="tpu_custom_call" | custom-call | flops 9126805504 | bytes 100663296 | tf_op jit(solution)/shard_map/model/pallas_call | solution.py:329
  178.9 0.9 convert_element_type.62
  179.8 3.5 %all-to-all-start.1 = ((bf16[16,64,128]{2,1,0:T(8,128)(2,1)}), bf16[16,64,128]{2,1,0:T(8,128)(2,1)S(1)}, u32[]{:S(2)}, u32[]{:S(2)}) async-start(bf16[16,64,128]{2,1,0:T(8,128)(2,1)} %bitcast.8), calls=%async_computation.1 | async-start | bytes 524288 | tf_op jit(solution)/shard_map/all_to_all | solution.py:483
  183.4 0.7 pad_convert_fusion.observed_ref
  184.1 6.1 %line_up.1 = f32[33,8,128]{2,1,0:T(8,128)} custom-call(s32[64]{0:T(128)} %copy-done.10, f32[64,8,128]{2,1,0:T(8,128)} %pad_convert_fusion.observed_ref), custom_call_target="tpu_custom_call" | custom-call | tf_op jit(solution)/shard_map/line_up/pallas_call | solution.py:178
  190.2 0.9 slice.28
  191.1 2.3 all-to-all-done.1
  193.5 13.5 %all_to_all.15 = bf16[16,64,128]{2,1,0:T(8,128)(2,1)S(1)} all-to-all(bf16[16,64,128]{2,1,0:T(8,128)(2,1)S(1)} %broadcast_in_dim.133), channel_id=1, replica_groups=mesh['parts'=2,'band'=16] {'band'}, dimensions={0} | all-to-all | bytes 524288 | tf_op jit(solution)/shard_map/all_to_all | solution.py:432
  207.2 5.8 %copy-done = bf16[256,256,128]{2,1,0:T(8,128)(2,1)S(1)} copy-done((bf16[256,256,128]{2,1,0:T(8,128)(2,1)S(1)}, bf16[256,256,128]{2,1,0:T(8,128)(2,1)}, u32[]{:S(2)}) %copy-start) | copy-done | bytes 16777240
  213.0 88.1 %gradient.1 = bf16[256,16384]{1,0:T(8,128)(2,1)} custom-call(s32[1088]{0:T(1024)S(1)} %broadcast_add_fusion.order_ref, s32[1032]{0:T(1024)S(1)} %pad.22.window_ref, s32[1032]{0:T(1024)S(1)} %pad.23.low_ref, s32[1032]{0:T(1024)S(1)} %pad.24.high_ref, s32[1032]{0:T(1024)S(1)} %pad.25.row_ref, s32[1032]{0:T(1024)S(1)} %pad.26.half_ref, ...), custom_call_target="tpu_custom_call" | custom-call | flops 18253611008 | bytes 100663296 | tf_op jit(solution)/shard_map/gradient/pallas_call | solution.py:391
  (62 shorter events, 3.8 us)
Async XLA Ops:
  6.5 134.3 %all-gather.2.cloned.1.call-start = ((), (), s32[]{:S(2)}) async-start(), calls=%async_computation.3 | async-start | bytes 17825792 | tf_op jit(solution)/shard_map/all_gather | solution.py:446
  7.3 1.6 copy-start.5
  8.9 59.5 %copy-start.10 = (s32[64]{0:T(128)}, s32[64]{0:T(128)S(1)}, u32[]{:S(2)}) copy-start(s32[64]{0:T(128)S(1)} %select_reduce_fusion.3.first_ref) | copy-start | bytes 772
  13.2 62.5 %all-to-all-start = ((s32[16,1,192]{2,1,0:T(1,128)}), s32[16,1,192]{2,1,0:T(1,128)S(1)}, u32[]{:S(2)}, u32[]{:S(2)}) async-start(s32[16,1,192]{2,1,0:T(1,128)} %reshape.314), calls=%async_computation | async-start | bytes 32768 | tf_op jit(solution)/shard_map/all_to_all | solution.py:432
  22.6 3.7 %copy-start.2 = (bf16[256,16384]{1,0:T(8,128)(2,1)S(1)}, bf16[256,16384]{1,0:T(8,128)(2,1)}, u32[]{:S(2)}) copy-start(bf16[256,16384]{1,0:T(8,128)(2,1)} %sky_ref.1) | copy-start | bytes 25165828
  26.3 0.9 copy-start.6
  27.2 0.8 copy-start.8
  28.1 0.8 copy-start.9
  47.5 28.1 %copy-start.3 = (bf16[64,256,256]{2,1,0:T(8,128)(2,1)}, bf16[64,256,256]{2,1,0:T(8,128)(2,1)S(1)}, u32[]{:S(2)}) copy-start(bf16[64,256,256]{2,1,0:T(8,128)(2,1)S(1)} %rows_forward.1.spectrum_ref) | copy-start | bytes 25165828
  80.9 3.4 %copy-start.4 = (bf16[64,256,256]{2,1,0:T(8,128)(2,1)S(1)}, bf16[64,256,256]{2,1,0:T(8,128)(2,1)}, u32[]{:S(2)}) copy-start(bf16[64,256,256]{2,1,0:T(8,128)(2,1)} %copy-done.3) | copy-start | bytes 25165828
  140.8 5.8 %copy-start.1 = (bf16[512,128,128]{2,1,0:T(8,128)(2,1)S(1)}, bf16[512,128,128]{2,1,0:T(8,128)(2,1)}, u32[]{:S(2)}) copy-start(bf16[512,128,128]{2,1,0:T(8,128)(2,1)} %all-gather.2.cloned.1.call-done.packed_ref) | copy-start | bytes 50331652
  146.6 36.8 %copy-start.13 = (bf16[64,2,128]{2,1,0:T(2,128)(2,1)S(1)}, bf16[64,2,128]{2,1,0:T(2,128)(2,1)}, u32[]{:S(2)}) copy-start(bf16[64,2,128]{2,1,0:T(2,128)(2,1)} %param.17) | copy-start | bytes 98308
  146.6 60.6 %copy-start.7 = (f32[256,128]{1,0:T(8,128)S(1)}, f32[256,128]{1,0:T(8,128)}, u32[]{:S(2)}) copy-start(f32[256,128]{1,0:T(8,128)} %constant.170.clone.twist_ref) | copy-start | bytes 393220
  146.6 60.6 %copy-start.11 = (bf16[256,128]{1,0:T(8,128)(2,1)S(1)}, bf16[256,128]{1,0:T(8,128)(2,1)}, u32[]{:S(2)}) copy-start(bf16[256,128]{1,0:T(8,128)(2,1)} %constant.171.clone.head_ref) | copy-start | bytes 196612
  146.6 60.6 %copy-start.12 = (bf16[128,256]{1,0:T(8,128)(2,1)S(1)}, bf16[128,256]{1,0:T(8,128)(2,1)}, u32[]{:S(2)}) copy-start(bf16[128,256]{1,0:T(8,128)(2,1)} %constant.172.clone.tail_ref) | copy-start | bytes 196612
  179.8 13.5 %all-to-all-start.1 = ((bf16[16,64,128]{2,1,0:T(8,128)(2,1)}), bf16[16,64,128]{2,1,0:T(8,128)(2,1)S(1)}, u32[]{:S(2)}, u32[]{:S(2)}) async-start(bf16[16,64,128]{2,1,0:T(8,128)(2,1)} %bitcast.8), calls=%async_computation.1 | async-start | bytes 524288 | tf_op jit(solution)/shard_map/all_to_all | solution.py:483
  207.2 5.8 %copy-start = (bf16[256,256,128]{2,1,0:T(8,128)(2,1)S(1)}, bf16[256,256,128]{2,1,0:T(8,128)(2,1)}, u32[]{:S(2)}) copy-start(bf16[256,256,128]{2,1,0:T(8,128)(2,1)} %subtract_convert_fusion.table_ref) | copy-start | bytes 50331652
Sparse Core Ops, SparseCore 0:
  11.3 129.5 all-gather.1

commit v5 on v3

--- a/solution.py
+++ b/solution.py
@@ -392,7 +392,7 @@
             pltpu.VMEM((2, ROWS_STEP, SIDE), BF16),
             pltpu.SemaphoreType.DMA((2,)),
         ],
-        compiler_params=pltpu.CompilerParams(vmem_limit_bytes=47 * MIB),
+        compiler_params=pltpu.CompilerParams(vmem_limit_bytes=31 * MIB),
         cost_estimate=pl.CostEstimate(flops=scalars[0].shape[0] * RADIX ** 3 * 8, bytes_accessed=96 * MIB, transcendentals=0),
         name="gradient",
     )(*scalars, table, residual, *inverse_tables(), packed)

time: 306 us -> 307 us (level)
  local copies, waits for them, and re-layouts: 20.8 us -> 26.6 us
  Pallas kernels: 183 us -> 178 us
    unnamed x28 -> x30, local copies, waits for them, and re-layouts: 17.9 us -> 23.6 us
    pallas_call x1, Pallas kernels: 91.4 us -> 86.6 us  [gradient_rows(): pl.pallas_call(gradient_kernel, in_specs=[pl.BlockSpec(memory_space=pltpu...]
where the time goes in v5:
time: 307 us
  Pallas kernels  178 us (58%)
  other arithmetic  36.4 us (12%)
  waiting for transfers between devices  27.4 us (9%)
  local copies, waits for them, and re-layouts  26.6 us (9%)
  between operations  14.4 us (5%)
  blocking collectives  13.5 us (4%)
  starting transfers between devices  10.9 us (4%)
    pallas_call x1, Pallas kernels, gradient_rows(): pl.pallas_call(gradient_kernel, in_specs=[pl.BlockSpec(memory_space=pltpu...  86.6 us
    pallas_call x1, Pallas kernels, model_parts(): pl.pallas_call(functools.partial(model_kernel, resident), in_specs=[pl.Bl...  32.8 us
    pallas_call x1, Pallas kernels, tile_parts(): pl.pallas_call(tiles_kernel, in_specs=[pl.BlockSpec(memory_space=pltpu.SM...  31.5 us
    all_gather x1, waiting for transfers between devices, on_device(): packed = lax.all_gather(pack(first, kernel, tiles_here), 'band', tiled=True)  25.1 us
    unnamed x30, local copies, waits for them, and re-layouts  23.6 us
    convert_element_type x1, other arithmetic, column_tables(): inverse.astype(BF16)  20.8 us
    pallas_call x1, Pallas kernels, rows_forward(): pl.pallas_call(rows_forward_kernel, grid=(rows // ROWS_STEP,), in_specs=[...  18.6 us
    all_to_all x1, blocking collectives, spread(): lax.all_to_all(jnp.broadcast_to(values[None], (band_count,) + values.shap...  13.5 us
  transfers between devices with their start and end apart: 3, of which 2 were waited for; matrix products, arithmetic and copies ran while one was open for 12% of the time, Pallas kernels for 18%

profile of v5, /device:TPU:0, one launch (start us, length us, event | category | flops | bytes accessed | tf_op | source)
XLA Modules:
  0.0 307.0 jit_solution(15372139822448759160)
XLA Ops:
  6.5 0.8 select_reduce_fusion.3.first_ref
  7.3 1.6 copy-done.5
  8.9 2.2 pack.1
  11.2 0.7 fusion.24
  11.8 0.7 pad_add_fusion
  12.5 0.7 reshape.314
  13.2 7.4 %all-to-all-start = ((s32[16,1,192]{2,1,0:T(1,128)}), s32[16,1,192]{2,1,0:T(1,128)S(1)}, u32[]{:S(2)}, u32[]{:S(2)}) async-start(s32[16,1,192]{2,1,0:T(1,128)} %reshape.314), calls=%async_computation | async-start | bytes 32768 | tf_op jit(solution)/shard_map/all_to_all | solution.py:423
  20.6 0.6 cosine_multiply_fusion
  21.6 1.0 fusion.13
  22.6 3.7 %copy-done.2 = bf16[256,16384]{1,0:T(8,128)(2,1)S(1)} copy-done((bf16[256,16384]{1,0:T(8,128)(2,1)S(1)}, bf16[256,16384]{1,0:T(8,128)(2,1)}, u32[]{:S(2)}) %copy-start.2) | copy-done | bytes 8388632
  26.3 0.9 copy-done.6
  27.2 0.8 copy-done.8
  28.1 0.8 copy-done.9
  28.9 18.6 %rows_forward.1.spectrum_ref = bf16[64,256,256]{2,1,0:T(8,128)(2,1)S(1)} custom-call(bf16[256,16384]{1,0:T(8,128)(2,1)S(1)} %copy-done.2, bf16[256,128]{1,0:T(8,128)(2,1)S(1)} %copy-done.8, f32[256,128]{1,0:T(8,128)S(1)} %copy-done.6, bf16[128,256]{1,0:T(8,128)(2,1)S(1)} %copy-done.9), custom_call_target="tpu_custom_call" | custom-call | flops 4294967296 | bytes 16777216 | tf_op jit(solution)/shard_map/rows_forward/pallas_call | solution.py:86
  47.5 20.8 %subtract_convert_fusion.table_ref = bf16[256,256,128]{2,1,0:T(8,128)(2,1)} fusion(f32[256,128]{1,0:T(8,128)S(1)} %bitcast.17, f32[256,256]{1,0:T(8,128)S(1)} %get-tuple-element.21, f32[256,128]{1,0:T(8,128)S(1)} %bitcast.16, f32[256,256]{1,0:T(8,128)S(1)} %get-tuple-element.20), kind=kLoop, calls=%fused_computation | loop fusion | flops 33554432 | bytes 17563648 | tf_op jit(solution)/shard_map/convert_element_type | solution.py:413
  68.4 7.2 %subtract_convert_fusion.1.table_ref = bf16[256,128,256]{2,1,0:T(8,128)(2,1)} fusion(f32[128,256]{1,0:T(8,128)S(1)} %copy.20, f32[256,256]{1,0:T(8,128)S(1)} %get-tuple-element.21, f32[128,256]{1,0:T(8,128)S(1)} %copy.19, f32[256,256]{1,0:T(8,128)S(1)} %get-tuple-element.20), kind=kLoop, calls=%fused_computation.1 | loop fusion | flops 33554432 | bytes 17563648 | tf_op jit(solution)/shard_map/convert_element_type | solution.py:413
  76.3 0.7 reduce.13
  77.6 0.7 slice.23
  80.9 3.4 %copy-done.4 = bf16[64,256,256]{2,1,0:T(8,128)(2,1)S(1)} copy-done((bf16[64,256,256]{2,1,0:T(8,128)(2,1)S(1)}, bf16[64,256,256]{2,1,0:T(8,128)(2,1)}, u32[]{:S(2)}) %copy-start.4) | copy-done | bytes 8388632
  84.3 31.5 %tiles.1.tiles_ref = bf16[1088,128,128]{2,1,0:T(8,128)(2,1)} custom-call(s32[1088]{0:T(1024)S(1)} %broadcast_add_fusion.order_ref, s32[1032]{0:T(1024)S(1)} %pad.25.row_ref, s32[544]{0:T(1024)S(1)} %broadcast_minimum_fusion.block_ref, s32[1]{0:T(128)S(6)} %select_n.115.steps_ref, bf16[256,128,256]{2,1,0:T(8,128)(2,1)} %subtract_convert_fusion.1.table_ref, ...), custom_call_target="tpu_custom_call" | custom-call | flops 18253611008 | bytes 67108864 | tf_op jit(solution)/shard_map/tiles/pallas_call | solution.py:221
  115.8 25.1 %all-gather.2.cloned.1.call-done.packed_ref = bf16[512,128,128]{2,1,0:T(8,128)(2,1)} async-done(((bf16[32,128,128]{2,1,0:T(8,128)(2,1)}), bf16[512,128,128]{2,1,0:T(8,128)(2,1)}) %all-gather.2.cloned.1.call-update) | async-done | bytes 16777232 | tf_op jit(solution)/shard_map/all_gather | solution.py:437
  140.8 5.8 %copy-done.1 = bf16[512,128,128]{2,1,0:T(8,128)(2,1)S(1)} copy-done((bf16[512,128,128]{2,1,0:T(8,128)(2,1)S(1)}, bf16[512,128,128]{2,1,0:T(8,128)(2,1)}, u32[]{:S(2)}) %copy-start.1) | copy-done | bytes 16777240
  146.6 32.8 %model.1 = f32[512,2,128]{2,1,0:T(2,128)S(1)} custom-call(s32[1088]{0:T(1024)S(1)} %broadcast_add_fusion.order_ref, s32[1032]{0:T(1024)S(1)} %pad.22.window_ref, s32[1032]{0:T(1024)S(1)} %pad.23.low_ref, s32[1032]{0:T(1024)S(1)} %pad.24.high_ref, s32[1032]{0:T(1024)S(1)} %pad.26.half_ref, s32[1]{0:T(128)S(6)} %select_n.115.steps_ref, ...), custom_call_target="tpu_custom_call" | custom-call | flops 9126805504 | bytes 100663296 | tf_op jit(solution)/shard_map/model/pallas_call | solution.py:329
  179.4 0.9 convert_element_type.62
  180.3 3.5 %all-to-all-start.1 = ((bf16[16,64,128]{2,1,0:T(8,128)(2,1)}), bf16[16,64,128]{2,1,0:T(8,128)(2,1)S(1)}, u32[]{:S(2)}, u32[]{:S(2)}) async-start(bf16[16,64,128]{2,1,0:T(8,128)(2,1)} %bitcast.8), calls=%async_computation.1 | async-start | bytes 524288 | tf_op jit(solution)/shard_map/all_to_all | solution.py:474
  183.9 0.7 pad_convert_fusion.observed_ref
  184.6 6.1 %line_up.1 = f32[33,8,128]{2,1,0:T(8,128)} custom-call(s32[64]{0:T(128)} %copy-done.10, f32[64,8,128]{2,1,0:T(8,128)} %pad_convert_fusion.observed_ref), custom_call_target="tpu_custom_call" | custom-call | tf_op jit(solution)/shard_map/line_up/pallas_call | solution.py:178
  190.7 0.9 slice.28
  191.6 2.3 all-to-all-done.1
  194.0 13.5 %all_to_all.15 = bf16[16,64,128]{2,1,0:T(8,128)(2,1)S(1)} all-to-all(bf16[16,64,128]{2,1,0:T(8,128)(2,1)S(1)} %broadcast_in_dim.133), channel_id=1, replica_groups=mesh['parts'=2,'band'=16] {'band'}, dimensions={0} | all-to-all | bytes 524288 | tf_op jit(solution)/shard_map/all_to_all | solution.py:423
  207.7 5.8 %copy-done = bf16[256,256,128]{2,1,0:T(8,128)(2,1)S(1)} copy-done((bf16[256,256,128]{2,1,0:T(8,128)(2,1)S(1)}, bf16[256,256,128]{2,1,0:T(8,128)(2,1)}, u32[]{:S(2)}) %copy-start) | copy-done | bytes 16777240
  213.5 86.6 %gradient.1 = bf16[256,16384]{1,0:T(8,128)(2,1)} custom-call(s32[1088]{0:T(1024)S(1)} %broadcast_add_fusion.order_ref, s32[1032]{0:T(1024)S(1)} %pad.22.window_ref, s32[1032]{0:T(1024)S(1)} %pad.23.low_ref, s32[1032]{0:T(1024)S(1)} %pad.24.high_ref, s32[1032]{0:T(1024)S(1)} %pad.25.row_ref, s32[1032]{0:T(1024)S(1)} %pad.26.half_ref, ...), custom_call_target="tpu_custom_call" | custom-call | flops 18253611008 | bytes 100663296 | tf_op jit(solution)/shard_map/gradient/pallas_call | solution.py:383
  (62 shorter events, 3.8 us)
Async XLA Ops:
  6.5 134.3 %all-gather.2.cloned.1.call-start = ((), (), s32[]{:S(2)}) async-start(), calls=%async_computation.3 | async-start | bytes 17825792 | tf_op jit(solution)/shard_map/all_gather | solution.py:437
  7.3 1.6 copy-start.5
  8.9 59.5 %copy-start.10 = (s32[64]{0:T(128)}, s32[64]{0:T(128)S(1)}, u32[]{:S(2)}) copy-start(s32[64]{0:T(128)S(1)} %select_reduce_fusion.3.first_ref) | copy-start | bytes 772
  13.2 62.5 %all-to-all-start = ((s32[16,1,192]{2,1,0:T(1,128)}), s32[16,1,192]{2,1,0:T(1,128)S(1)}, u32[]{:S(2)}, u32[]{:S(2)}) async-start(s32[16,1,192]{2,1,0:T(1,128)} %reshape.314), calls=%async_computation | async-start | bytes 32768 | tf_op jit(solution)/shard_map/all_to_all | solution.py:423
  22.6 3.7 %copy-start.2 = (bf16[256,16384]{1,0:T(8,128)(2,1)S(1)}, bf16[256,16384]{1,0:T(8,128)(2,1)}, u32[]{:S(2)}) copy-start(bf16[256,16384]{1,0:T(8,128)(2,1)} %sky_ref.1) | copy-start | bytes 25165828
  26.3 0.9 copy-start.6
  27.2 0.8 copy-start.8
  28.1 0.8 copy-start.9
  47.5 28.1 %copy-start.3 = (bf16[64,256,256]{2,1,0:T(8,128)(2,1)}, bf16[64,256,256]{2,1,0:T(8,128)(2,1)S(1)}, u32[]{:S(2)}) copy-start(bf16[64,256,256]{2,1,0:T(8,128)(2,1)S(1)} %rows_forward.1.spectrum_ref) | copy-start | bytes 25165828
  80.9 3.4 %copy-start.4 = (bf16[64,256,256]{2,1,0:T(8,128)(2,1)S(1)}, bf16[64,256,256]{2,1,0:T(8,128)(2,1)}, u32[]{:S(2)}) copy-start(bf16[64,256,256]{2,1,0:T(8,128)(2,1)} %copy-done.3) | copy-start | bytes 25165828
  140.8 5.8 %copy-start.1 = (bf16[512,128,128]{2,1,0:T(8,128)(2,1)S(1)}, bf16[512,128,128]{2,1,0:T(8,128)(2,1)}, u32[]{:S(2)}) copy-start(bf16[512,128,128]{2,1,0:T(8,128)(2,1)} %all-gather.2.cloned.1.call-done.packed_ref) | copy-start | bytes 50331652
  146.6 37.2 %copy-start.13 = (bf16[64,2,128]{2,1,0:T(2,128)(2,1)S(1)}, bf16[64,2,128]{2,1,0:T(2,128)(2,1)}, u32[]{:S(2)}) copy-start(bf16[64,2,128]{2,1,0:T(2,128)(2,1)} %param.17) | copy-start | bytes 98308
  146.6 61.1 %copy-start.7 = (f32[256,128]{1,0:T(8,128)S(1)}, f32[256,128]{1,0:T(8,128)}, u32[]{:S(2)}) copy-start(f32[256,128]{1,0:T(8,128)} %constant.170.clone.twist_ref) | copy-start | bytes 393220
  146.6 61.1 %copy-start.11 = (bf16[256,128]{1,0:T(8,128)(2,1)S(1)}, bf16[256,128]{1,0:T(8,128)(2,1)}, u32[]{:S(2)}) copy-start(bf16[256,128]{1,0:T(8,128)(2,1)} %constant.171.clone.head_ref) | copy-start | bytes 196612
  146.6 61.1 %copy-start.12 = (bf16[128,256]{1,0:T(8,128)(2,1)S(1)}, bf16[128,256]{1,0:T(8,128)(2,1)}, u32[]{:S(2)}) copy-start(bf16[128,256]{1,0:T(8,128)(2,1)} %constant.172.clone.tail_ref) | copy-start | bytes 196612
  180.3 13.5 %all-to-all-start.1 = ((bf16[16,64,128]{2,1,0:T(8,128)(2,1)}), bf16[16,64,128]{2,1,0:T(8,128)(2,1)S(1)}, u32[]{:S(2)}, u32[]{:S(2)}) async-start(bf16[16,64,128]{2,1,0:T(8,128)(2,1)} %bitcast.8), calls=%async_computation.1 | async-start | bytes 524288 | tf_op jit(solution)/shard_map/all_to_all | solution.py:474
  207.7 5.8 %copy-start = (bf16[256,256,128]{2,1,0:T(8,128)(2,1)S(1)}, bf16[256,256,128]{2,1,0:T(8,128)(2,1)}, u32[]{:S(2)}) copy-start(bf16[256,256,128]{2,1,0:T(8,128)(2,1)} %subtract_convert_fusion.table_ref) | copy-start | bytes 50331652
Sparse Core Ops, SparseCore 0:
  11.3 129.5 all-gather.1
